TPU v7x, 32 devices: a whole 2x2x4 slice. The times are simulated.
32 devices in a mesh: group: 2 (over core), gx: 4 (over y, x), gy: 4 (over z).
Axes of the slice: x: 2, y: 2, z: 4, core: 2. Of those that a mesh axis runs over, the one named last changes fastest.
Arguments:
- start_vectors: float32 [2, 4, 4, 8, 384, 128], P('group', 'gx', 'gy')
- tile_blocks: bfloat16 [2, 4, 4, 8, 4, 384, 384], P('group', 'gx', 'gy')
- block_columns: int32 [2, 4, 4, 8, 4], P('group', 'gx', 'gy'), may hold values from 0 to 11, as said below
- sleeve_rod: int32 [4, 4, 1, 4, 8], P('gx', 'gy'), may hold values from -1 to 511, as said below
- sleeve_membrane: int32 [4, 4, 1, 4, 8], P('gx', None, None, 'gy'), may hold values from -1 to 511, as said below
- sleeve_stiffness: float32 [4, 4, 1, 4, 8], P('gx', None, None, 'gy'), may hold values from 0.25 to 4
Outputs:
- final_vectors: float32 [2, 4, 4, 8, 384, 128], P('group', 'gx', 'gy')
- norms: float32 [3, 128], replicated
Inputs may be any that keep to these rules, and one draw needn't show every extreme that they name: `block_columns`: entry 0 of block row r is r itself; every other entry names one of the device's 8 blocks, or 8 to 11 for the west, east, south and north ghost blocks. sleeve_rod[x, y, m, y2, :] lists the nodes of rod device (0, x, y) tied to membrane tile (m + 1, x, y2); -1 marks an empty slot and live slots come first. In every draw one membrane tile receives 8 live slots from each of the 4 rod devices of its column. `sleeve_membrane`: -1 at exactly the slots where sleeve_rod is -1; elsewhere a node of membrane tile (m + 1, x, y2).
All inputs are finite; a program needn't handle non-finite values.
Results may differ from a plain program's by a relative error of at most 0.005.
Values may be sent and summed in bfloat16 or wider, within the bound.
A program may use at most 64 MiB of HBM per device.

v0:
```python
import jax
import jax.numpy as jnp
from jax import lax
from jax.sharding import PartitionSpec as P

MATVECS = 3


epsilon = 1e-06


def extended_2(shard, sides, width):
    for axis, dim in sides:
        count, length = (lax.axis_size(axis), shard.shape[dim])
        up = [(i, (i + 1) % count) for i in range(count - 1)]
        down = [(j, i) for i, j in up]
        last = lax.slice_in_dim(shard, length - width, length, axis=dim)
        initial = lax.slice_in_dim(shard, 0, width, axis=dim)
        before = lax.ppermute(last, axis, up)
        after = lax.ppermute(initial, axis, down)
        shard = jnp.concatenate([before, shard, after], axis=dim)
    return shard


def local(start_vectors, tile_blocks, block_columns, sleeve_rod, sleeve_membrane, sleeve_stiffness):
    n_blocks = tile_blocks.shape[3]
    width = tile_blocks.shape[5]
    vectors = start_vectors.shape[5]
    capacity = sleeve_rod.shape[4]
    groups = lax.axis_size("group")
    rows_y = lax.axis_size("gy")
    nodes = n_blocks * width // 6
    payload = 6 * vectors
    all_dofs = float(groups * lax.axis_size("gx") * rows_y * n_blocks * width)
    group_index = lax.axis_index("group")
    rod_flag = group_index == 0
    membrane_flag = (group_index > 0).astype(jnp.float32)
    blocks = tile_blocks[0, 0, 0]
    columns = block_columns[0, 0, 0].reshape(-1)
    send_nodes = sleeve_rod[0, 0].reshape(-1)
    send_live = (send_nodes >= 0) & rod_flag
    send_safe = jnp.maximum(send_nodes, 0)
    node_ids = jnp.arange(nodes, dtype=jnp.int32)
    rod_gather = jnp.where(
        (node_ids[:, None] == send_nodes[None, :]) & rod_flag, jnp.float32(1.0), jnp.float32(0.0)
    )
    memb_slot = jnp.maximum(group_index - 1, 0)
    recv_nodes = lax.dynamic_index_in_dim(
        sleeve_membrane[0, :, :, 0, :], memb_slot, axis=1, keepdims=False
    ).reshape(-1)
    recv_stiff = lax.dynamic_index_in_dim(
        sleeve_stiffness[0, :, :, 0, :], memb_slot, axis=1, keepdims=False
    ).reshape(-1)
    recv_live = (recv_nodes >= 0).astype(jnp.float32) * membrane_flag
    recv_safe = jnp.maximum(recv_nodes, 0)
    weighted = (
        jnp.where(node_ids[:, None] == recv_nodes[None, :], recv_stiff[None, :], jnp.float32(0.0))
        * membrane_flag
    )
    node_weight = jnp.sum(weighted, axis=1)
    slot_stiff = recv_stiff * recv_live
    current = start_vectors[0, 0, 0]
    norms = []
    for matvec in range(MATVECS):
        rounded = current.astype(jnp.bfloat16)
        edges_x = jnp.stack([rounded[0], rounded[n_blocks - 1]])
        padded_x = extended_2(edges_x, (("gx", 0),), 1)
        edges_y = jnp.stack([rounded[n_blocks - 2], rounded[1]])
        padded_y = extended_2(edges_y, (("gy", 0),), 1)
        extended = jnp.concatenate(
            [rounded, padded_x[0:1], padded_x[3:4], padded_y[0:1], padded_y[3:4]], axis=0
        )
        picked = jnp.take(extended, columns, axis=0).reshape(n_blocks, -1, width, vectors)
        product = jnp.einsum("rkij,rkjs->ris", blocks, picked, preferred_element_type=jnp.float32)
        node_rows = rounded.reshape(nodes, payload)
        outgoing = jnp.where(
            send_live[:, None], jnp.take(node_rows, send_safe, axis=0), jnp.zeros((), jnp.bfloat16)
        )
        outgoing = outgoing.reshape(groups - 1, rows_y, capacity, payload)
        outgoing = jnp.concatenate(
            [jnp.zeros((1, rows_y, capacity, payload), jnp.bfloat16), outgoing], axis=0
        )
        arrived = lax.all_to_all(
            outgoing.reshape(groups * rows_y, capacity, payload),
            ("group", "gy"),
            split_axis=0,
            concat_axis=0,
            tiled=True,
        )[:rows_y]
        arrived = arrived.reshape(rows_y * capacity, payload).astype(jnp.float32)
        pulled = jnp.dot(weighted, arrived, precision=lax.Precision.HIGHEST)
        coupling = node_weight[:, None] * node_rows.astype(jnp.float32) - pulled
        memb_at_slot = jnp.take(node_rows, recv_safe, axis=0).astype(jnp.float32)
        delta = (slot_stiff[:, None] * (memb_at_slot - arrived)).astype(jnp.bfloat16)
        back = delta.reshape(1, rows_y, capacity, payload)
        back = jnp.concatenate(
            [back, jnp.zeros((groups - 1, rows_y, capacity, payload), jnp.bfloat16)], axis=0
        )
        returned = lax.all_to_all(
            back.reshape(groups * rows_y, capacity, payload),
            ("group", "gy"),
            split_axis=0,
            concat_axis=0,
            tiled=True,
        )
        returned = (
            returned.reshape(groups, rows_y * capacity, payload)[1:]
            .reshape(-1, payload)
            .astype(jnp.float32)
        )
        pushed = jnp.dot(rod_gather, returned, precision=lax.Precision.HIGHEST)
        coupling = coupling - pushed
        coupled = product + coupling.reshape(n_blocks, width, vectors)
        squares = lax.psum(jnp.sum(coupled * coupled, axis=(0, 1)), ("group", "gx", "gy"))
        scale = jnp.sqrt(squares / all_dofs + epsilon)
        current = coupled / scale
        norms.append(scale)
    return (current[None, None, None], jnp.stack(norms))


def solution(mesh):
    return jax.shard_map(
        local,
        mesh=mesh,
        in_specs=(
            P("group", "gx", "gy", None, None, None),
            P("group", "gx", "gy", None, None, None, None),
            P("group", "gx", "gy", None, None),
            P("gx", "gy", None, None, None),
            P("gx", None, None, "gy", None),
            P("gx", None, None, "gy", None),
        ),
        out_specs=(P("group", "gx", "gy", None, None, None), P()),
        check_vma=False,
    )
```

profile of v0, /device:TPU:0, one launch (start us, length us, event | category | flops | bytes accessed | tf_op | source)
XLA Modules:
  0.0 298.0 jit_solution(12773748503910134570)
XLA Ops:
  5.3 6.3 %all-to-all-start = ((bf16[8,8,768]{2,1,0:T(8,128)(2,1)}), bf16[8,8,768]{2,1,0:T(8,128)(2,1)S(1)}, u32[]{:S(2)}, u32[]{:S(2)}) async-start(bf16[8,8,768]{2,1,0:T(8,128)(2,1)} %bitcast.11), calls=%async_computation | async-start | bytes 196608 | tf_op jit(solution)/shard_map/all_to_all | solution.py:83
  12.9 4.6 %collective-permute-start.2 = (bf16[1,384,128]{2,1,0:T(8,128)(2,1)S(1)}, bf16[1,384,128]{2,1,0:T(8,128)(2,1)S(1)}, u32[]{:S(2)}, u32[]{:S(2)}) collective-permute-start(bf16[1,384,128]{2,1,0:T(8,128)(2,1)S(1)} %get-tuple-element.25), channel_id=1, source_target_pairs={{0,1},{1,2},{2,3},{4,5},{5,6},{6,7},{8,9},{9,10},{10,11},{12,13},{... | collective-permute-start | bytes 294920 | tf_op jit(solution)/shard_map/ppermute | solution.py:19
  18.8 4.6 %collective-permute-start = (bf16[1,384,128]{2,1,0:T(8,128)(2,1)S(1)}, bf16[1,384,128]{2,1,0:T(8,128)(2,1)S(1)}, u32[]{:S(2)}, u32[]{:S(2)}) collective-permute-start(bf16[1,384,128]{2,1,0:T(8,128)(2,1)S(1)} %get-tuple-element.27), channel_id=1, source_target_pairs={{0,4},{4,8},{8,12},{1,5},{5,9},{9,13},{2,6},{6,10},{10,14},{3,7},{... | collective-permute-start | bytes 294920 | tf_op jit(solution)/shard_map/ppermute | solution.py:19
  32.6 4.2 %all-to-all-start.1 = ((bf16[8,8,768]{2,1,0:T(8,128)(2,1)}), bf16[8,8,768]{2,1,0:T(8,128)(2,1)S(1)}, u32[]{:S(2)}, u32[]{:S(2)}) async-start(bf16[8,8,768]{2,1,0:T(8,128)(2,1)} %bitcast.14), calls=%async_computation.1 | async-start | bytes 196608 | tf_op jit(solution)/shard_map/all_to_all | solution.py:99
  38.8 4.4 %all-to-all-done.1 = bf16[8,8,768]{2,1,0:T(8,128)(2,1)S(1)} async-done(((bf16[8,8,768]{2,1,0:T(8,128)(2,1)}), bf16[8,8,768]{2,1,0:T(8,128)(2,1)S(1)}, u32[]{:S(2)}, u32[]{:S(2)}) %all-to-all-start.1) | async-done | bytes 98336 | tf_op jit(solution)/shard_map/all_to_all | solution.py:99
  43.3 3.9 %subtract_subtract_fusion.2 = f32[512,768]{1,0:T(8,128)} fusion(f32[512,768]{1,0:T(8,128)} %fusion.17, bf16[512,768]{1,0:T(8,128)(2,1)} %copy-done, f32[512]{0:T(512)S(1)} %fusion.18, bf16[8,8,768]{2,1,0:T(8,128)(2,1)S(1)} %all-to-all-done.1, s32[32]{0:T(128)S(1)} %reshape_squeeze.7, pred[]{:T(512)S(6)} %eq.35), kind=kOutput, calls=%fused_computation.29 | convolution fusion | flops 152616960 | bytes 3983873 | tf_op jit(solution)/shard_map/dot_general | solution.py:111
  52.6 8.2 %multiply_reduce_fusion.2 = (f32[128]{0:T(128)S(1)}, f32[8,384,128]{1,2,0:T(8,128)}) fusion(f32[8,384,128]{1,2,0:T(8,128)} %copy.24, bf16[8,4,384,128]{3,2,1,0:T(8,128)(2,1)S(1)} %bitcast.104, bf16[1,1,1,8,4,384,384]{6,5,4,3,2,1,0:T(8,128)(2,1)} %param.11), kind=kOutput, calls=%fused_computation.28 | convolution fusion | flops 1209139072 | bytes 15729152 | tf_op jit(solution)/shard_map/rkij,rkjs->ris/dot_general | solution.py:74
  60.8 39.0 %psum.21 = f32[128]{0:T(128)S(1)} all-reduce(f32[128]{0:T(128)S(1)} %get-tuple-element.36), channel_id=1, replica_groups=mesh['group'=2,'gx'=4,'gy'=4] {'group','gx','gy'}, use_global_device_ids=true, to_apply=%region_2.5 | all-reduce | flops 128 | bytes 1024 | tf_op jit(solution)/shard_map/psum | solution.py:114
  103.4 4.2 %collective-permute-start.4 = (bf16[1,384,128]{1,2,0:T(8,128)(2,1)S(1)}, bf16[1,384,128]{1,2,0:T(8,128)(2,1)S(1)}, u32[]{:S(2)}, u32[]{:S(2)}) collective-permute-start(bf16[1,384,128]{1,2,0:T(8,128)(2,1)S(1)} %get-tuple-element.23), channel_id=1, source_target_pairs={{0,4},{4,8},{8,12},{1,5},{5,9},{9,13},{2,6},{6,10},{10,14},{3,7},{... | collective-permute-start | bytes 294920 | tf_op jit(solution)/shard_map/ppermute | solution.py:19
  113.6 4.6 %collective-permute-start.6 = (bf16[1,384,128]{1,2,0:T(8,128)(2,1)S(1)}, bf16[1,384,128]{1,2,0:T(8,128)(2,1)S(1)}, u32[]{:S(2)}, u32[]{:S(2)}) collective-permute-start(bf16[1,384,128]{1,2,0:T(8,128)(2,1)S(1)} %get-tuple-element.21), channel_id=1, source_target_pairs={{0,1},{1,2},{2,3},{4,5},{5,6},{6,7},{8,9},{9,10},{10,11},{12,13},{... | collective-permute-start | bytes 294920 | tf_op jit(solution)/shard_map/ppermute | solution.py:19
  119.5 5.2 %collective-permute-done.5 = bf16[1,384,128]{1,2,0:T(8,128)(2,1)S(1)} collective-permute-done((bf16[1,384,128]{1,2,0:T(8,128)(2,1)S(1)}, bf16[1,384,128]{1,2,0:T(8,128)(2,1)S(1)}, u32[]{:S(2)}, u32[]{:S(2)}) %collective-permute-start.5) | collective-permute-done | bytes 98336 | tf_op jit(solution)/shard_map/ppermute | solution.py:20
  130.5 4.1 %all-to-all-start.3 = ((bf16[8,8,768]{2,1,0:T(8,128)(2,1)}), bf16[8,8,768]{2,1,0:T(8,128)(2,1)S(1)}, u32[]{:S(2)}, u32[]{:S(2)}) async-start(bf16[8,8,768]{2,1,0:T(8,128)(2,1)} %bitcast.24), calls=%async_computation.3 | async-start | bytes 196608 | tf_op jit(solution)/shard_map/all_to_all | solution.py:99
  136.6 4.4 %all-to-all-done.3 = bf16[8,8,768]{2,1,0:T(8,128)(2,1)S(1)} async-done(((bf16[8,8,768]{2,1,0:T(8,128)(2,1)}), bf16[8,8,768]{2,1,0:T(8,128)(2,1)S(1)}, u32[]{:S(2)}, u32[]{:S(2)}) %all-to-all-start.3) | async-done | bytes 98336 | tf_op jit(solution)/shard_map/all_to_all | solution.py:99
  141.1 3.9 %subtract_subtract_fusion.1 = f32[512,768]{1,0:T(8,128)} fusion(f32[512,768]{1,0:T(8,128)} %fusion.16, bf16[512,768]{1,0:T(8,128)(2,1)} %copy-done.2, f32[512]{0:T(512)S(1)} %fusion.18, bf16[8,8,768]{2,1,0:T(8,128)(2,1)S(1)} %all-to-all-done.3, s32[32]{0:T(128)S(1)} %reshape_squeeze.7, pred[]{:T(512)S(6)} %eq.35), kind=kOutput, calls=%fused_computation.26 | convolution fusion | flops 152616960 | bytes 3983873 | tf_op jit(solution)/shard_map/dot_general | solution.py:111
  150.4 8.1 %multiply_reduce_fusion.1 = (f32[128]{0:T(128)S(1)}, f32[8,384,128]{1,2,0:T(8,128)}) fusion(f32[8,384,128]{1,2,0:T(8,128)} %copy.26, bf16[8,4,384,128]{2,3,1,0:T(8,128)(2,1)S(1)} %bitcast.106, bf16[1,1,1,8,4,384,384]{6,5,4,3,2,1,0:T(8,128)(2,1)} %param.11), kind=kOutput, calls=%fused_computation.25 | convolution fusion | flops 1209139072 | bytes 15729152 | tf_op jit(solution)/shard_map/rkij,rkjs->ris/dot_general | solution.py:74
  158.5 38.5 %psum.22 = f32[128]{0:T(128)S(1)} all-reduce(f32[128]{0:T(128)S(1)} %get-tuple-element.38), channel_id=1, replica_groups=mesh['group'=2,'gx'=4,'gy'=4] {'group','gx','gy'}, use_global_device_ids=true, to_apply=%region_4.7 | all-reduce | flops 128 | bytes 1024 | tf_op jit(solution)/shard_map/psum | solution.py:114
  200.6 4.2 %collective-permute-start.8 = (bf16[1,384,128]{1,2,0:T(8,128)(2,1)S(1)}, bf16[1,384,128]{1,2,0:T(8,128)(2,1)S(1)}, u32[]{:S(2)}, u32[]{:S(2)}) collective-permute-start(bf16[1,384,128]{1,2,0:T(8,128)(2,1)S(1)} %get-tuple-element.19), channel_id=1, source_target_pairs={{0,4},{4,8},{8,12},{1,5},{5,9},{9,13},{2,6},{6,10},{10,14},{3,7},{... | collective-permute-start | bytes 294920 | tf_op jit(solution)/shard_map/ppermute | solution.py:19
  210.8 4.6 %collective-permute-start.10 = (bf16[1,384,128]{1,2,0:T(8,128)(2,1)S(1)}, bf16[1,384,128]{1,2,0:T(8,128)(2,1)S(1)}, u32[]{:S(2)}, u32[]{:S(2)}) collective-permute-start(bf16[1,384,128]{1,2,0:T(8,128)(2,1)S(1)} %get-tuple-element.17), channel_id=1, source_target_pairs={{0,1},{1,2},{2,3},{4,5},{5,6},{6,7},{8,9},{9,10},{10,11},{12,13},{... | collective-permute-start | bytes 294920 | tf_op jit(solution)/shard_map/ppermute | solution.py:19
  216.7 5.2 %collective-permute-done.9 = bf16[1,384,128]{1,2,0:T(8,128)(2,1)S(1)} collective-permute-done((bf16[1,384,128]{1,2,0:T(8,128)(2,1)S(1)}, bf16[1,384,128]{1,2,0:T(8,128)(2,1)S(1)}, u32[]{:S(2)}, u32[]{:S(2)}) %collective-permute-start.9) | collective-permute-done | bytes 98336 | tf_op jit(solution)/shard_map/ppermute | solution.py:20
  227.7 4.1 %all-to-all-start.5 = ((bf16[8,8,768]{2,1,0:T(8,128)(2,1)}), bf16[8,8,768]{2,1,0:T(8,128)(2,1)S(1)}, u32[]{:S(2)}, u32[]{:S(2)}) async-start(bf16[8,8,768]{2,1,0:T(8,128)(2,1)} %bitcast.34), calls=%async_computation.5 | async-start | bytes 196608 | tf_op jit(solution)/shard_map/all_to_all | solution.py:99
  233.8 4.4 %all-to-all-done.5 = bf16[8,8,768]{2,1,0:T(8,128)(2,1)S(1)} async-done(((bf16[8,8,768]{2,1,0:T(8,128)(2,1)}), bf16[8,8,768]{2,1,0:T(8,128)(2,1)S(1)}, u32[]{:S(2)}, u32[]{:S(2)}) %all-to-all-start.5) | async-done | bytes 98336 | tf_op jit(solution)/shard_map/all_to_all | solution.py:99
  238.2 3.9 %subtract_subtract_fusion = f32[512,768]{1,0:T(8,128)} fusion(f32[512,768]{1,0:T(8,128)} %fusion.15, bf16[512,768]{1,0:T(8,128)(2,1)} %copy-done.1, f32[512]{0:T(512)S(1)} %fusion.18, bf16[8,8,768]{2,1,0:T(8,128)(2,1)S(1)} %all-to-all-done.5, s32[32]{0:T(128)S(1)} %reshape_squeeze.7, pred[]{:T(512)S(6)} %eq.35), kind=kOutput, calls=%fused_computation.23 | convolution fusion | flops 152616960 | bytes 3983873 | tf_op jit(solution)/shard_map/dot_general | solution.py:111
  247.6 8.1 %multiply_reduce_fusion = (f32[128]{0:T(128)S(1)}, f32[8,384,128]{1,2,0:T(8,128)}) fusion(f32[8,384,128]{1,2,0:T(8,128)} %copy.28, bf16[8,4,384,128]{2,3,1,0:T(8,128)(2,1)S(1)} %bitcast.105, bf16[1,1,1,8,4,384,384]{6,5,4,3,2,1,0:T(8,128)(2,1)} %param.11), kind=kOutput, calls=%fused_computation.22 | convolution fusion | flops 1209139072 | bytes 15729152 | tf_op jit(solution)/shard_map/rkij,rkjs->ris/dot_general | solution.py:74
  255.7 38.5 %psum.23 = f32[128]{0:T(128)S(1)} all-reduce(f32[128]{0:T(128)S(1)} %get-tuple-element.40), channel_id=1, replica_groups=mesh['group'=2,'gx'=4,'gy'=4] {'group','gx','gy'}, use_global_device_ids=true, to_apply=%region_6.9 | all-reduce | flops 128 | bytes 1024 | tf_op jit(solution)/shard_map/psum | solution.py:114
  (115 shorter events, 75.8 us)
Async XLA Ops:
  3.2 20.7 %copy-start.4 = (s32[1,4,1,1,8]{4,3,2,1,0:T(1,128)S(1)}, s32[1,4,1,1,8]{4,3,2,1,0:T(1,128)}, u32[]{:S(2)}) copy-start(s32[1,4,1,1,8]{4,3,2,1,0:T(1,128)} %param.14) | copy-start | bytes 388
  3.2 22.0 %copy-start.5 = (f32[1,4,1,1,8]{4,3,2,1,0:T(1,128)S(1)}, f32[1,4,1,1,8]{4,3,2,1,0:T(1,128)}, u32[]{:S(2)}) copy-start(f32[1,4,1,1,8]{4,3,2,1,0:T(1,128)} %param.15) | copy-start | bytes 388
  3.2 22.8 %copy-start.3 = (s32[1,1,1,8,4]{3,4,2,1,0:T(4,128)S(1)}, s32[1,1,1,8,4]{3,4,2,1,0:T(4,128)}, u32[]{:S(2)}) copy-start(s32[1,1,1,8,4]{3,4,2,1,0:T(4,128)} %param.12) | copy-start | bytes 388
  3.9 23.1 %copy-start = (bf16[512,768]{1,0:T(8,128)(2,1)}, bf16[512,768]{1,0:T(8,128)(2,1)S(1)}, u32[]{:S(2)}) copy-start(bf16[512,768]{1,0:T(8,128)(2,1)S(1)} %convert_element_type.62) | copy-start | bytes 2359300
  5.3 26.6 %all-to-all-start = ((bf16[8,8,768]{2,1,0:T(8,128)(2,1)}), bf16[8,8,768]{2,1,0:T(8,128)(2,1)S(1)}, u32[]{:S(2)}, u32[]{:S(2)}) async-start(bf16[8,8,768]{2,1,0:T(8,128)(2,1)} %bitcast.11), calls=%async_computation | async-start | bytes 196608 | tf_op jit(solution)/shard_map/all_to_all | solution.py:83
  11.6 15.3 %collective-permute-start.3 = (bf16[1,384,128]{2,1,0:T(8,128)(2,1)S(1)}, bf16[1,384,128]{2,1,0:T(8,128)(2,1)S(1)}, u32[]{:S(2)}, u32[]{:S(2)}) collective-permute-start(bf16[1,384,128]{2,1,0:T(8,128)(2,1)S(1)} %get-tuple-element.24), channel_id=1, source_target_pairs={{1,0},{2,1},{3,2},{5,4},{6,5},{7,6},{9,8},{10,9},{11,10},{13,12},{... | collective-permute-start | bytes 294920 | tf_op jit(solution)/shard_map/ppermute | solution.py:20
  12.9 14.0 %collective-permute-start.2 = (bf16[1,384,128]{2,1,0:T(8,128)(2,1)S(1)}, bf16[1,384,128]{2,1,0:T(8,128)(2,1)S(1)}, u32[]{:S(2)}, u32[]{:S(2)}) collective-permute-start(bf16[1,384,128]{2,1,0:T(8,128)(2,1)S(1)} %get-tuple-element.25), channel_id=1, source_target_pairs={{0,1},{1,2},{2,3},{4,5},{5,6},{6,7},{8,9},{9,10},{10,11},{12,13},{... | collective-permute-start | bytes 294920 | tf_op jit(solution)/shard_map/ppermute | solution.py:19
  17.5 9.4 %collective-permute-start.1 = (bf16[1,384,128]{2,1,0:T(8,128)(2,1)S(1)}, bf16[1,384,128]{2,1,0:T(8,128)(2,1)S(1)}, u32[]{:S(2)}, u32[]{:S(2)}) collective-permute-start(bf16[1,384,128]{2,1,0:T(8,128)(2,1)S(1)} %get-tuple-element.26), channel_id=1, source_target_pairs={{4,0},{8,4},{12,8},{5,1},{9,5},{13,9},{6,2},{10,6},{14,10},{7,3},{... | collective-permute-start | bytes 294920 | tf_op jit(solution)/shard_map/ppermute | solution.py:20
  18.8 8.1 %collective-permute-start = (bf16[1,384,128]{2,1,0:T(8,128)(2,1)S(1)}, bf16[1,384,128]{2,1,0:T(8,128)(2,1)S(1)}, u32[]{:S(2)}, u32[]{:S(2)}) collective-permute-start(bf16[1,384,128]{2,1,0:T(8,128)(2,1)S(1)} %get-tuple-element.27), channel_id=1, source_target_pairs={{0,4},{4,8},{8,12},{1,5},{5,9},{9,13},{2,6},{6,10},{10,14},{3,7},{... | collective-permute-start | bytes 294920 | tf_op jit(solution)/shard_map/ppermute | solution.py:19
  32.6 10.7 %all-to-all-start.1 = ((bf16[8,8,768]{2,1,0:T(8,128)(2,1)}), bf16[8,8,768]{2,1,0:T(8,128)(2,1)S(1)}, u32[]{:S(2)}, u32[]{:S(2)}) async-start(bf16[8,8,768]{2,1,0:T(8,128)(2,1)} %bitcast.14), calls=%async_computation.1 | async-start | bytes 196608 | tf_op jit(solution)/shard_map/all_to_all | solution.py:99
  102.7 22.0 %copy-start.2 = (bf16[512,768]{1,0:T(8,128)(2,1)}, bf16[512,768]{1,0:T(8,128)(2,1)S(1)}, u32[]{:S(2)}) copy-start(bf16[512,768]{1,0:T(8,128)(2,1)S(1)} %reshape.150) | copy-start | bytes 2359300
  103.4 16.1 %collective-permute-start.4 = (bf16[1,384,128]{1,2,0:T(8,128)(2,1)S(1)}, bf16[1,384,128]{1,2,0:T(8,128)(2,1)S(1)}, u32[]{:S(2)}, u32[]{:S(2)}) collective-permute-start(bf16[1,384,128]{1,2,0:T(8,128)(2,1)S(1)} %get-tuple-element.23), channel_id=1, source_target_pairs={{0,4},{4,8},{8,12},{1,5},{5,9},{9,13},{2,6},{6,10},{10,14},{3,7},{... | collective-permute-start | bytes 294920 | tf_op jit(solution)/shard_map/ppermute | solution.py:19
  109.0 20.8 %all-to-all-start.2 = ((bf16[8,8,768]{2,1,0:T(8,128)(2,1)}), bf16[8,8,768]{2,1,0:T(8,128)(2,1)S(1)}, u32[]{:S(2)}, u32[]{:S(2)}) async-start(bf16[8,8,768]{2,1,0:T(8,128)(2,1)} %bitcast.21), calls=%async_computation.2 | async-start | bytes 196608 | tf_op jit(solution)/shard_map/all_to_all | solution.py:83
  112.3 12.4 %collective-permute-start.7 = (bf16[1,384,128]{1,2,0:T(8,128)(2,1)S(1)}, bf16[1,384,128]{1,2,0:T(8,128)(2,1)S(1)}, u32[]{:S(2)}, u32[]{:S(2)}) collective-permute-start(bf16[1,384,128]{1,2,0:T(8,128)(2,1)S(1)} %get-tuple-element.20), channel_id=1, source_target_pairs={{1,0},{2,1},{3,2},{5,4},{6,5},{7,6},{9,8},{10,9},{11,10},{13,12},{... | collective-permute-start | bytes 294920 | tf_op jit(solution)/shard_map/ppermute | solution.py:20
  113.6 11.1 %collective-permute-start.6 = (bf16[1,384,128]{1,2,0:T(8,128)(2,1)S(1)}, bf16[1,384,128]{1,2,0:T(8,128)(2,1)S(1)}, u32[]{:S(2)}, u32[]{:S(2)}) collective-permute-start(bf16[1,384,128]{1,2,0:T(8,128)(2,1)S(1)} %get-tuple-element.21), channel_id=1, source_target_pairs={{0,1},{1,2},{2,3},{4,5},{5,6},{6,7},{8,9},{9,10},{10,11},{12,13},{... | collective-permute-start | bytes 294920 | tf_op jit(solution)/shard_map/ppermute | solution.py:19
  118.2 6.5 %collective-permute-start.5 = (bf16[1,384,128]{1,2,0:T(8,128)(2,1)S(1)}, bf16[1,384,128]{1,2,0:T(8,128)(2,1)S(1)}, u32[]{:S(2)}, u32[]{:S(2)}) collective-permute-start(bf16[1,384,128]{1,2,0:T(8,128)(2,1)S(1)} %get-tuple-element.22), channel_id=1, source_target_pairs={{4,0},{8,4},{12,8},{5,1},{9,5},{13,9},{6,2},{10,6},{14,10},{7,3},{... | collective-permute-start | bytes 294920 | tf_op jit(solution)/shard_map/ppermute | solution.py:20
  130.5 10.6 %all-to-all-start.3 = ((bf16[8,8,768]{2,1,0:T(8,128)(2,1)}), bf16[8,8,768]{2,1,0:T(8,128)(2,1)S(1)}, u32[]{:S(2)}, u32[]{:S(2)}) async-start(bf16[8,8,768]{2,1,0:T(8,128)(2,1)} %bitcast.24), calls=%async_computation.3 | async-start | bytes 196608 | tf_op jit(solution)/shard_map/all_to_all | solution.py:99
  199.9 22.0 %copy-start.1 = (bf16[512,768]{1,0:T(8,128)(2,1)}, bf16[512,768]{1,0:T(8,128)(2,1)S(1)}, u32[]{:S(2)}) copy-start(bf16[512,768]{1,0:T(8,128)(2,1)S(1)} %reshape.159) | copy-start | bytes 2359300
  200.6 16.1 %collective-permute-start.8 = (bf16[1,384,128]{1,2,0:T(8,128)(2,1)S(1)}, bf16[1,384,128]{1,2,0:T(8,128)(2,1)S(1)}, u32[]{:S(2)}, u32[]{:S(2)}) collective-permute-start(bf16[1,384,128]{1,2,0:T(8,128)(2,1)S(1)} %get-tuple-element.19), channel_id=1, source_target_pairs={{0,4},{4,8},{8,12},{1,5},{5,9},{9,13},{2,6},{6,10},{10,14},{3,7},{... | collective-permute-start | bytes 294920 | tf_op jit(solution)/shard_map/ppermute | solution.py:19
  206.1 20.8 %all-to-all-start.4 = ((bf16[8,8,768]{2,1,0:T(8,128)(2,1)}), bf16[8,8,768]{2,1,0:T(8,128)(2,1)S(1)}, u32[]{:S(2)}, u32[]{:S(2)}) async-start(bf16[8,8,768]{2,1,0:T(8,128)(2,1)} %bitcast.31), calls=%async_computation.4 | async-start | bytes 196608 | tf_op jit(solution)/shard_map/all_to_all | solution.py:83
  209.5 12.4 %collective-permute-start.11 = (bf16[1,384,128]{1,2,0:T(8,128)(2,1)S(1)}, bf16[1,384,128]{1,2,0:T(8,128)(2,1)S(1)}, u32[]{:S(2)}, u32[]{:S(2)}) collective-permute-start(bf16[1,384,128]{1,2,0:T(8,128)(2,1)S(1)} %get-tuple-element.16), channel_id=1, source_target_pairs={{1,0},{2,1},{3,2},{5,4},{6,5},{7,6},{9,8},{10,9},{11,10},{13,12},{... | collective-permute-start | bytes 294920 | tf_op jit(solution)/shard_map/ppermute | solution.py:20
  210.8 11.1 %collective-permute-start.10 = (bf16[1,384,128]{1,2,0:T(8,128)(2,1)S(1)}, bf16[1,384,128]{1,2,0:T(8,128)(2,1)S(1)}, u32[]{:S(2)}, u32[]{:S(2)}) collective-permute-start(bf16[1,384,128]{1,2,0:T(8,128)(2,1)S(1)} %get-tuple-element.17), channel_id=1, source_target_pairs={{0,1},{1,2},{2,3},{4,5},{5,6},{6,7},{8,9},{9,10},{10,11},{12,13},{... | collective-permute-start | bytes 294920 | tf_op jit(solution)/shard_map/ppermute | solution.py:19
  215.4 6.5 %collective-permute-start.9 = (bf16[1,384,128]{1,2,0:T(8,128)(2,1)S(1)}, bf16[1,384,128]{1,2,0:T(8,128)(2,1)S(1)}, u32[]{:S(2)}, u32[]{:S(2)}) collective-permute-start(bf16[1,384,128]{1,2,0:T(8,128)(2,1)S(1)} %get-tuple-element.18), channel_id=1, source_target_pairs={{4,0},{8,4},{12,8},{5,1},{9,5},{13,9},{6,2},{10,6},{14,10},{7,3},{... | collective-permute-start | bytes 294920 | tf_op jit(solution)/shard_map/ppermute | solution.py:20
  227.7 10.6 %all-to-all-start.5 = ((bf16[8,8,768]{2,1,0:T(8,128)(2,1)}), bf16[8,8,768]{2,1,0:T(8,128)(2,1)S(1)}, u32[]{:S(2)}, u32[]{:S(2)}) async-start(bf16[8,8,768]{2,1,0:T(8,128)(2,1)} %bitcast.34), calls=%async_computation.5 | async-start | bytes 196608 | tf_op jit(solution)/shard_map/all_to_all | solution.py:99
where the time goes:
time: 300 us; the launch traced here: 298 us
  blocking collectives  116 us (39%)
  starting transfers between devices  59.8 us (20%)
  matrix products  42.2 us (14%)
  local copies, waits for them, and re-layouts  39 us (13%)
  waiting for transfers between devices  23.7 us (8%)
  other arithmetic  16.2 us (5%)
    psum x3, blocking collectives, local(): lax.psum(jnp.sum(coupled * coupled, axis=(0, 1)), ('group', 'gx', 'gy'))  116 us
    ppermute x6, starting transfers between devices, extended_2(): before = lax.ppermute(last, axis, up)  26.6 us
    dot_general x3, matrix products, local(): jnp.einsum('rkij,rkjs->ris', blocks, picked, preferred_element_type=jnp.f...  24.4 us
    reshape x6, local copies, waits for them, and re-layouts, local(): coupled = product + coupling.reshape(n_blocks, width, vectors)  16.5 us
    all_to_all x3, waiting for transfers between devices, local(): lax.all_to_all(back.reshape(groups * rows_y, capacity, payload), ('group'...  13.3 us
    all_to_all x3, starting transfers between devices, local(): lax.all_to_all(outgoing.reshape(groups * rows_y, capacity, payload), ('gr...  13 us
    all_to_all x3, starting transfers between devices, local(): lax.all_to_all(back.reshape(groups * rows_y, capacity, payload), ('group'...  12.4 us
    dot_general x3, matrix products, local(): pushed = jnp.dot(rod_gather, returned, precision=lax.Precision.HIGHEST)  11.6 us
  transfers between devices with their start and end apart: 18, of which 5 were waited for; matrix products, arithmetic and copies ran while one was open for 9% of the time, Pallas kernels for 0%

commit v1 on v0

v1 whole, which is shorter than its diff:
```python
import functools

import jax
import jax.numpy as jnp
from jax import lax
from jax.experimental import pallas as pl
from jax.experimental.pallas import tpu as pltpu
from jax.sharding import PartitionSpec as P

MATVECS = 3
DOFS = 6
EPSILON = 1e-06
MESH = pl.DeviceIdType.MESH
F32 = jnp.float32
BF16 = jnp.bfloat16


def kernel(groups, gxs, gys, nb, kb, width, lanes, rows,
           cols, idx_col, idx_row, kap_col, v_hbm, a_hbm,
           out_hbm, norms,
           a, ext_0, ext_1, ext_2, v32, acc0, c3, gat, sca, own, oth, kown, kap, dlt, sqacc, sqa, sqb, inv,
           v_sem, a0_sem, a_sem, o_sem, gs, gr, ss, sr, ks, kr, as_, ar, bs, br):
    ext = (ext_0, ext_1, ext_2)
    g = lax.axis_index("group")
    x = lax.axis_index("gx")
    y = lax.axis_index("gy")
    plane = g * gxs + x
    rod = g == 0
    members = groups - 1
    chunks = members * gys
    all_dofs = float(groups * gxs * gys * nb * width)

    def row_of(i):
        half, odd = lax.div(i, 2), lax.rem(i, 2)
        return half * (1 - 2 * odd) + odd * (nb - 1)

    order = [i // 2 if i % 2 == 0 else nb - 1 - i // 2 for i in range(nb)]
    for r in order:
        pltpu.make_async_copy(v_hbm.at[r], v32.at[r], v_sem.at[r]).start()
    pltpu.make_async_copy(a_hbm.at[:, 0], a.at[:, 0], a0_sem).start()
    for r in order:
        pltpu.make_async_copy(a_hbm.at[r, pl.ds(1, kb - 1)], a.at[r, pl.ds(1, kb - 1)], a_sem.at[r]).start()

    barrier = pltpu.get_barrier_semaphore()
    for i in range(gys):
        @pl.when(i != y)
        def _():
            pl.semaphore_signal(barrier, inc=1, device_id=(g, x, i), device_id_type=MESH)
    for p in range(groups * gxs):
        @pl.when(p != plane)
        def _():
            pl.semaphore_signal(barrier, inc=1, device_id=(p // gxs, p % gxs, y), device_id_type=MESH)

    def peer(c):
        return (jnp.where(rod, c // gys + 1, 0), x, c % gys)

    def each_chunk(body):
        for c in range(chunks):
            if c < gys:
                body(c)
            else:
                pl.when(rod)(functools.partial(body, c))

    each_chunk(lambda c: pl.semaphore_signal(barrier, inc=1, device_id=peer(c), device_id_type=MESH))

    sides = (
        (nb - 1, x < gxs - 1, lambda: (g, x + 1, y), x > 0, lambda: (g, x - 1, y)),
        (0, x > 0, lambda: (g, x - 1, y), x < gxs - 1, lambda: (g, x + 1, y)),
        (1, y < gys - 1, lambda: (g, x, y + 1), y > 0, lambda: (g, x, y - 1)),
        (nb - 2, y > 0, lambda: (g, x, y - 1), y < gys - 1, lambda: (g, x, y + 1)),
    )
    for d, (_, _, _, hears, _) in enumerate(sides):
        @pl.when(jnp.logical_not(hears))
        def _():
            for s in range(MATVECS):
                ext[s][nb + d] = jnp.zeros((width, lanes), BF16)

    kown[...] = jnp.broadcast_to(kap_col[...], (gys * rows, lanes)).reshape(gys, rows, lanes)

    @pl.when(jnp.logical_not(rod))
    def _():
        kap[0] = kown[...]
        for m in range(1, members):
            kap[m] = jnp.zeros((gys, rows, lanes), F32)
            for s in range(MATVECS):
                oth[s, m] = jnp.zeros((gys, rows, lanes), BF16)

    def gather_matrix(m, carry):
        for r in range(nb):
            dof = lax.broadcasted_iota(jnp.int32, (gys * rows, width), 1) + r * width
            hot = jnp.where(idx_col[m] == dof, F32(1.0), F32(0.0)).astype(BF16)
            gat[m, :, r * width:(r + 1) * width] = hot
        return carry

    lax.fori_loop(0, members, gather_matrix, 0)

    for r in order[:4]:
        pltpu.make_async_copy(v_hbm.at[r], v32.at[r], v_sem.at[r]).wait()
        ext[0][r] = v32[r].astype(BF16)

    pl.semaphore_wait(barrier, gys - 1 + groups * gxs - 1 + jnp.where(rod, chunks, gys))

    def side_copy(s, d, device):
        return pltpu.make_async_remote_copy(
            src_ref=ext[s].at[sides[d][0]], dst_ref=ext[s].at[nb + d],
            send_sem=gs.at[s, d], recv_sem=gr.at[s, d],
            device_id=device, device_id_type=MESH)

    def send_sides(s):
        for d, (_, sends, to, _, _) in enumerate(sides):
            @pl.when(sends)
            def _():
                side_copy(s, d, to()).start()

    def wait_sides(s):
        for d, (_, _, _, hears, source) in enumerate(sides):
            @pl.when(hears)
            def _():
                side_copy(s, d, source()).wait_recv()

    my_chunk = jnp.where(rod, y, (g - 1) * gys + y)

    def sleeve_copy(s, c, dst):
        return pltpu.make_async_remote_copy(
            src_ref=own.at[s, c // gys, c % gys], dst_ref=oth.at[s, dst // gys, dst % gys],
            send_sem=ss.at[s, c], recv_sem=sr.at[s, dst],
            device_id=peer(c), device_id_type=MESH)

    def kap_copy(c, dst):
        return pltpu.make_async_remote_copy(
            src_ref=kown.at[c % gys], dst_ref=kap.at[dst // gys, dst % gys],
            send_sem=ks.at[c % gys], recv_sem=kr.at[dst],
            device_id=peer(c), device_id_type=MESH)

    send_sides(0)

    @pl.when(jnp.logical_not(rod))
    def _():
        for c in range(gys):
            kap_copy(c, my_chunk).start()

    for r in order[4:]:
        pltpu.make_async_copy(v_hbm.at[r], v32.at[r], v_sem.at[r]).wait()
        ext[0][r] = v32[r].astype(BF16)

    def gather(s):
        def one(m, carry):
            got = jnp.dot(gat[m], ext[s][:nb].reshape(nb * width, lanes), preferred_element_type=F32)
            own[s, m] = got.astype(BF16).reshape(gys, rows, lanes)
            return carry

        lax.fori_loop(0, members, one, 0)
        each_chunk(lambda c: sleeve_copy(s, c, my_chunk).start())

    def first_blocks(s):
        def one(r, carry):
            acc0[r] = jnp.dot(a[r, 0], ext[s][r], preferred_element_type=F32)
            return carry

        lax.fori_loop(0, nb, one, 0)

    def spring_forces(s):
        each_chunk(lambda c: sleeve_copy(s, c, c).wait_recv())
        for m in range(members):
            force = kap[m] * (own[s, m].astype(F32) - oth[s, m].astype(F32))
            dlt[m * gys * rows:(m + 1) * gys * rows] = force.astype(BF16).reshape(gys * rows, lanes)

    def main_rows(s, start, stop):
        def one(i, carry):
            r = row_of(i)
            if s == 0:
                pltpu.make_async_copy(
                    a_hbm.at[r, pl.ds(1, kb - 1)], a.at[r, pl.ds(1, kb - 1)], a_sem.at[r]).wait()
            left = jnp.concatenate([a[r, k] for k in range(1, kb)] + [sca[r]], axis=1)
            right = jnp.concatenate([ext[s][cols[r * kb + k]] for k in range(1, kb)] + [dlt[...]], axis=0)
            c = acc0[r] + jnp.dot(left, right, preferred_element_type=F32)
            if s > 0:
                c = c * inv[...]
            sqacc[...] += jnp.sum((c * c).reshape(width // 8, 8, lanes), axis=0)
            if s < MATVECS - 1:
                ext[s + 1][r] = c.astype(BF16)
            else:
                c3[r] = c
                pltpu.make_async_copy(c3.at[r], out_hbm.at[r], o_sem.at[r]).start()
            return carry

        lax.fori_loop(start, stop, one, 0)

    def line_copy(s, i, slot):
        return pltpu.make_async_remote_copy(
            src_ref=sqa.at[s, y], dst_ref=sqa.at[s, slot],
            send_sem=as_.at[s, i], recv_sem=ar.at[s, slot],
            device_id=(g, x, i), device_id_type=MESH)

    def plane_copy(s, p, slot):
        return pltpu.make_async_remote_copy(
            src_ref=sqb.at[s, plane], dst_ref=sqb.at[s, slot],
            send_sem=bs.at[s, p], recv_sem=br.at[s, slot],
            device_id=(p // gxs, p % gxs, y), device_id_type=MESH)

    def squares_line(s):
        sqa[s, y] = sqacc[...]
        for i in range(gys):
            @pl.when(i != y)
            def _():
                line_copy(s, i, y).start()

    def squares_plane(s):
        for i in range(gys):
            @pl.when(i != y)
            def _():
                line_copy(s, i, i).wait_recv()
        total = sqa[s, 0]
        for i in range(1, gys):
            total = total + sqa[s, i]
        sqb[s, plane] = total
        for p in range(groups * gxs):
            @pl.when(p != plane)
            def _():
                plane_copy(s, p, plane).start()

    def squares_end(s):
        for p in range(groups * gxs):
            @pl.when(p != plane)
            def _():
                plane_copy(s, p, p).wait_recv()
        total = sqb[s, 0]
        for p in range(1, groups * gxs):
            total = total + sqb[s, p]
        scale = jnp.sqrt(jnp.sum(total, axis=0, keepdims=True) / all_dofs + EPSILON)
        norms[s:s + 1, :] = scale
        inv[...] = 1.0 / scale

    for s in range(MATVECS):
        gather(s)
        if s == 0:
            def scatter_matrix(r, carry):
                dof = lax.broadcasted_iota(jnp.int32, (width, sca.shape[2]), 0) + r * width
                sca[r] = jnp.where(idx_row[...] == dof, F32(1.0), F32(0.0)).astype(BF16)
                return carry

            lax.fori_loop(0, nb, scatter_matrix, 0)
            if dlt.shape[0] > chunks * rows:
                dlt[chunks * rows:] = jnp.zeros((dlt.shape[0] - chunks * rows, lanes), BF16)
            pltpu.make_async_copy(a_hbm.at[:, 0], a.at[:, 0], a0_sem).wait()
        first_blocks(s)
        if s > 0:
            squares_plane(s - 1)
        else:
            @pl.when(rod)
            def _():
                for c in range(chunks):
                    kap_copy(c, c).wait_recv()
        spring_forces(s)
        wait_sides(s)
        if s > 0:
            squares_end(s - 1)
        sqacc[...] = jnp.zeros_like(sqacc)
        main_rows(s, 0, 4)
        if s < MATVECS - 1:
            send_sides(s + 1)
        main_rows(s, 4, nb)
        squares_line(s)
    squares_plane(MATVECS - 1)
    for s in range(MATVECS):
        for d, (_, sends, to, _, _) in enumerate(sides):
            @pl.when(sends)
            def _():
                side_copy(s, d, to()).wait_send()
        each_chunk(lambda c: sleeve_copy(s, c, c).wait_send())
        for i in range(gys):
            @pl.when(i != y)
            def _():
                line_copy(s, i, y).wait_send()

    @pl.when(jnp.logical_not(rod))
    def _():
        for c in range(gys):
            kap_copy(c, c).wait_send()

    for r in range(nb):
        pltpu.make_async_copy(c3.at[r], out_hbm.at[r], o_sem.at[r]).wait()
    squares_end(MATVECS - 1)
    for s in range(MATVECS):
        for p in range(groups * gxs):
            @pl.when(p != plane)
            def _():
                plane_copy(s, p, plane).wait_send()


def local(groups, gxs, gys, start_vectors, tile_blocks, block_columns, sleeve_rod, sleeve_membrane, sleeve_stiffness):
    nb, kb, width = tile_blocks.shape[3:6]
    lanes = start_vectors.shape[5]
    cap = sleeve_rod.shape[4]
    members = groups - 1
    rows = cap * DOFS
    chunks = members * gys
    slot_rows = chunks * rows
    padded = -(-slot_rows // 256) * 256
    g = lax.axis_index("group")
    member = jnp.maximum(g - 1, 0)
    memb = lax.dynamic_index_in_dim(sleeve_membrane[0, :, :, 0, :], member, axis=1, keepdims=False).reshape(-1)
    stiff = lax.dynamic_index_in_dim(sleeve_stiffness[0, :, :, 0, :], member, axis=1, keepdims=False).reshape(-1)
    memb = jnp.pad(memb, (0, (members - 1) * gys * cap), constant_values=-1)
    nodes = jnp.where(g == 0, sleeve_rod[0, 0].reshape(-1), memb)
    index = jnp.where(nodes[:, None] >= 0, nodes[:, None] * DOFS + jnp.arange(DOFS, dtype=jnp.int32)[None, :], -1)
    index = index.reshape(-1)
    idx_col = index.reshape(members, gys * rows, 1)
    idx_row = jnp.pad(index, (0, padded - slot_rows), constant_values=-1).reshape(1, padded)
    kap_col = jnp.broadcast_to(stiff[:, None], (gys * cap, DOFS)).reshape(gys * rows, 1)
    vmem = pl.BlockSpec(memory_space=pltpu.VMEM)
    hbm = pl.BlockSpec(memory_space=pl.ANY)
    dma = pltpu.SemaphoreType.DMA
    plane = groups * gxs
    flops = 2 * MATVECS * nb * kb * width * width * lanes
    coupled, norms = pl.pallas_call(
        functools.partial(kernel, groups, gxs, gys, nb, kb, width, lanes, rows),
        out_shape=(
            jax.ShapeDtypeStruct((nb, width, lanes), F32),
            jax.ShapeDtypeStruct((MATVECS, lanes), F32),
        ),
        in_specs=[pl.BlockSpec(memory_space=pltpu.SMEM), vmem, vmem, vmem, hbm, hbm],
        out_specs=(hbm, vmem),
        scratch_shapes=[
            pltpu.VMEM((nb, kb, width, width), BF16),
            *[pltpu.VMEM((nb + 4, width, lanes), BF16)] * MATVECS,
            pltpu.VMEM((nb, width, lanes), F32),
            pltpu.VMEM((nb, width, lanes), F32),
            pltpu.VMEM((nb, width, lanes), F32),
            pltpu.VMEM((members, gys * rows, nb * width), BF16),
            pltpu.VMEM((nb, width, padded), BF16),
            pltpu.VMEM((MATVECS, members, gys, rows, lanes), BF16),
            pltpu.VMEM((MATVECS, members, gys, rows, lanes), BF16),
            pltpu.VMEM((gys, rows, lanes), F32),
            pltpu.VMEM((members, gys, rows, lanes), F32),
            pltpu.VMEM((padded, lanes), BF16),
            pltpu.VMEM((8, lanes), F32),
            pltpu.VMEM((MATVECS, gys, 8, lanes), F32),
            pltpu.VMEM((MATVECS, plane, 8, lanes), F32),
            pltpu.VMEM((1, lanes), F32),
            dma((nb,)), dma, dma((nb,)), dma((nb,)),
            dma((MATVECS, 4)), dma((MATVECS, 4)),
            dma((MATVECS, chunks)), dma((MATVECS, chunks)),
            dma((gys,)), dma((chunks,)),
            dma((MATVECS, gys)), dma((MATVECS, gys)),
            dma((MATVECS, plane)), dma((MATVECS, plane)),
        ],
        compiler_params=pltpu.CompilerParams(
            collective_id=0, has_side_effects=True, vmem_limit_bytes=60 * 2**20),
        cost_estimate=pl.CostEstimate(flops=flops, bytes_accessed=tile_blocks.size * 2, transcendentals=0),
    )(block_columns.reshape(-1), idx_col, idx_row, kap_col,
      start_vectors.reshape(nb, width, lanes), tile_blocks.reshape(nb, kb, width, width))
    final = coupled / norms[MATVECS - 1]
    return (final[None, None, None], norms)


def solution(mesh):
    return jax.shard_map(
        functools.partial(local, mesh.shape["group"], mesh.shape["gx"], mesh.shape["gy"]),
        mesh=mesh,
        in_specs=(
            P("group", "gx", "gy", None, None, None),
            P("group", "gx", "gy", None, None, None, None),
            P("group", "gx", "gy", None, None),
            P("gx", "gy", None, None, None),
            P("gx", None, None, "gy", None),
            P("gx", None, None, "gy", None),
        ),
        out_specs=(P("group", "gx", "gy", None, None, None), P()),
        check_vma=False,
    )
```

time: 300 us -> 60.2 us (0.20)
  blocking collectives: 116 us -> 0 us
  starting transfers between devices: 59.8 us -> 0 us
  Pallas kernels: 0 us -> 46.9 us
  matrix products: 42.2 us -> 0 us
  local copies, waits for them, and re-layouts: 39 us -> 6.84 us
  waiting for transfers between devices: 23.7 us -> 0 us
  other arithmetic: 16.2 us -> 5.44 us
    psum x3 -> x0, blocking collectives: 116 us -> none  [local(): lax.psum(jnp.sum(coupled * coupled, axis=(0, 1)), ('group', 'gx', 'gy'))]
    pallas_call x0 -> x1, Pallas kernels: none -> 46.9 us  [local(): pl.pallas_call(functools.partial(kernel, groups, gxs, gys, nb, kb, width,...]
    dot_general x9 -> x0, matrix products: 42.2 us -> none  [the longest x3 24.4 us: local(): jnp.einsum('rkij,rkjs->ris', blocks, picked, preferred_element_type=jnp.f...]
    ppermute x12 -> x0, starting transfers between devices: 34.3 us -> none  [the longest x6 26.6 us: extended_2(): before = lax.ppermute(last, axis, up)]
    all_to_all x6 -> x0, starting transfers between devices: 25.4 us -> none  [the longest x3 13 us: local(): lax.all_to_all(outgoing.reshape(groups * rows_y, capacity, payload), ('gr...]
    reshape x8 -> x3, local copies, waits for them, and re-layouts: 17.9 us -> 1.46 us  [the longest x1 0.72 us: local(): jnp.broadcast_to(stiff[:, None], (gys * cap, DOFS)).reshape(gys * rows, 1)]
    all_to_all x6 -> x0, waiting for transfers between devices: 13.3 us -> none  [the longest x3 13.3 us: local(): lax.all_to_all(back.reshape(groups * rows_y, capacity, payload), ('group'...]
    gather x9 -> x0, local copies, waits for them, and re-layouts: 11.7 us -> none  [the longest x3 7.89 us: local(): jnp.take(extended, columns, axis=0).reshape(n_blocks, -1, width, vectors)]
  transfers between devices with their start and end apart: 18 -> 0, of which waited for: 5 -> 0; matrix products, arithmetic and copies ran while one was open for 9% -> 0% of each run, Pallas kernels for 0% -> 0%
where the time goes in v1:
time: 60.2 us; the launch traced here: 59.8 us
  Pallas kernels  46.9 us (78%)
  local copies, waits for them, and re-layouts  6.84 us (11%)
  other arithmetic  5.44 us (9%)
  between operations  0.66 us (1%)
    pallas_call x1, Pallas kernels, local(): pl.pallas_call(functools.partial(kernel, groups, gxs, gys, nb, kb, width,...  46.9 us
    unnamed x2, other arithmetic  2.69 us
    broadcast_in_dim x1, other arithmetic, local(): return (final[None, None, None], norms)  2.66 us
    unnamed x6, local copies, waits for them, and re-layouts  2.36 us

profile of v1, /device:TPU:0, one launch (start us, length us, event | category | flops | bytes accessed | tf_op | source)
XLA Modules:
  0.0 59.8 jit_solution(13338211909792891842)
XLA Ops:
  0.6 0.8 %reshape_squeeze.3 = s32[32]{0:T(128)S(1)} reshape(s32[1,1,1,4,8]{4,3,2,1,0:T(4,128)} %param.9) | data formatting | bytes 256 | tf_op jit(solution)/shard_map/reshape;squeeze | solution.py:305
  1.4 0.5 broadcast.46
  1.9 1.3 %reduce.6 = s32[4,8]{1,0:T(4,128)S(1)} reduce(s32[1,4,1,1,8]{4,3,2,1,0:T(1,128)} %param.10, s32[]{:T(128)} %broadcast.46), dimensions={0,2,3}, to_apply=%param.10.reduce_sub_computation.3 | reduce | bytes 260 | tf_op args[4]
  3.3 0.1 reshape.91
  3.4 0.5 broadcast.47
  3.9 1.3 %reduce.7 = f32[4,8]{1,0:T(4,128)S(1)} reduce(f32[1,4,1,1,8]{4,3,2,1,0:T(1,128)} %param.11, f32[]{:T(128)} %broadcast.47), dimensions={0,2,3}, to_apply=%param.11.reduce_sub_computation.3 | reduce | bytes 260 | tf_op args[5]
  5.2 0.1 broadcast_in_dim.27
  5.3 0.8 %copy.9 = s32[1,1,1,8,4]{4,3,2,1,0:T(8,128)S(1)} copy(s32[1,1,1,8,4]{3,4,2,1,0:T(4,128)} %param.8) | data formatting | bytes 256 | tf_op args[2]
  6.1 0.7 %reshape.90.cols = s32[32]{0:T(128)} reshape(s32[1,1,1,8,4]{4,3,2,1,0:T(8,128)S(1)} %copy.9) | data formatting | bytes 256 | tf_op jit(solution)/shard_map/reshape | solution.py:351
  6.7 0.1 add_select_fusion
  6.8 0.1 select_n.41
  6.9 0.6 pad.4
  7.5 0.1 broadcast_in_dim.28
  7.5 0.7 %reshape.96.kap_col = f32[192,1]{1,0:T(8,128)} reshape(f32[32,6]{1,0:T(8,128)S(1)} %broadcast_in_dim.28) | data formatting | bytes 1536 | tf_op jit(solution)/shard_map/reshape | solution.py:310
  8.3 0.7 %select_n.42.idx_col = s32[1,192,1]{2,1,0:T(8,128)} reshape(s32[32,6]{1,0:T(8,128)S(1)} %add_select_fusion) | data formatting | bytes 1536 | tf_op jit(solution)/shard_map/jit(_where)/select_n | solution.py:306
  9.0 46.9 %shard_map.77 = (f32[8,384,128]{2,1,0:T(8,128)}, f32[3,128]{1,0:T(4,128)}) custom-call(s32[32]{0:T(128)} %reshape.90.cols, s32[1,192,1]{2,1,0:T(8,128)} %select_n.42.idx_col, s32[1,256]{1,0:T(1,128)} %bitcast.9, f32[192,1]{1,0:T(8,128)} %reshape.96.kap_col, f32[8,384,128]{2,1,0:T(8,128)} %bitcast.11, bf16[8,4,384,384]{3,2,1,0:T(8,128)(2,1)} %bitcast.10), custom_call_target="tpu_custom_call" | custom-call | flops 3623878656 | bytes 9437184 | tf_op jit(solution)/shard_map/pallas_call | solution.py:316
  55.9 0.7 %slice_bitcast_fusion = f32[128]{0:T(128)S(1)} fusion(f32[3,128]{1,0:T(4,128)} %get-tuple-element.9), kind=kLoop, calls=%fused_computation.3 | loop fusion | bytes 1024 | tf_op jit(solution)/shard_map/div | solution.py:353
  56.6 0.0 copy-start
  56.6 2.7 %divide_bitcast_fusion = f32[1,1,1,8,384,128]{5,4,3,2,1,0:T(8,128)} fusion(f32[8,384,128]{2,1,0:T(8,128)} %get-tuple-element.4, f32[128]{0:T(128)S(1)} %slice_bitcast_fusion), kind=kLoop, calls=%fused_computation | loop fusion | flops 393216 | bytes 3146240 | tf_op jit(solution)/shard_map/broadcast_in_dim | solution.py:354
  59.3 0.0 copy-done
  59.3 0.6 copy.13
  (2 shorter events, 0.0 us)
Async XLA Ops:
  56.6 2.7 %copy-start = (f32[3,128]{1,0:T(4,128)S(1)}, f32[3,128]{1,0:T(4,128)}, u32[]{:S(2)}) copy-start(f32[3,128]{1,0:T(4,128)} %get-tuple-element.9) | copy-start | bytes 4612

commit v2 on v1

--- a/solution.py
+++ b/solution.py
@@ -16,10 +16,10 @@
 
 
 def kernel(groups, gxs, gys, nb, kb, width, lanes, rows,
-           cols, idx_col, idx_row, kap_col, v_hbm, a_hbm,
-           out_hbm, norms,
-           a, ext_0, ext_1, ext_2, v32, acc0, c3, gat, sca, own, oth, kown, kap, dlt, sqacc, sqa, sqb, inv,
-           v_sem, a0_sem, a_sem, o_sem, gs, gr, ss, sr, ks, kr, as_, ar, bs, br):
+           cols, rod_nodes, memb_nodes, stiff, v_hbm, a_hbm,
+           c3, norms, inverse,
+           a, ext_0, ext_1, ext_2, acc0, gat, sca, own, oth, kown, kap, dlt, sqacc, sqa, sqb, inv,
+           v_sem, a0_sem, a_sem, gs, gr, ss, sr, ks, kr, as_, ar, bs, br):
     ext = (ext_0, ext_1, ext_2)
     g = lax.axis_index("group")
     x = lax.axis_index("gx")
@@ -36,7 +36,7 @@
 
     order = [i // 2 if i % 2 == 0 else nb - 1 - i // 2 for i in range(nb)]
     for r in order:
-        pltpu.make_async_copy(v_hbm.at[r], v32.at[r], v_sem.at[r]).start()
+        pltpu.make_async_copy(v_hbm.at[r], acc0.at[r], v_sem.at[r]).start()
     pltpu.make_async_copy(a_hbm.at[:, 0], a.at[:, 0], a0_sem).start()
     for r in order:
         pltpu.make_async_copy(a_hbm.at[r, pl.ds(1, kb - 1)], a.at[r, pl.ds(1, kb - 1)], a_sem.at[r]).start()
@@ -75,7 +75,15 @@
             for s in range(MATVECS):
                 ext[s][nb + d] = jnp.zeros((width, lanes), BF16)
 
-    kown[...] = jnp.broadcast_to(kap_col[...], (gys * rows, lanes)).reshape(gys, rows, lanes)
+    cap = rows // DOFS
+    member = jnp.maximum(g - 1, 0)
+    slot = lax.broadcasted_iota(jnp.int32, (cap, lanes), 0)
+    for c in range(gys):
+        value = jnp.zeros((cap, lanes), F32)
+        for t in range(cap):
+            value = jnp.where(slot == t, stiff[c, member, 0, t], value)
+        for d in range(DOFS):
+            kown[c, d * cap:(d + 1) * cap] = value
 
     @pl.when(jnp.logical_not(rod))
     def _():
@@ -85,18 +93,27 @@
             for s in range(MATVECS):
                 oth[s, m] = jnp.zeros((gys, rows, lanes), BF16)
 
+    def node_of(m, c, t):
+        return jnp.where(rod, rod_nodes[m, c, t], jnp.where(m == 0, memb_nodes[c, member, 0, t], -1))
+
     def gather_matrix(m, carry):
-        for r in range(nb):
-            dof = lax.broadcasted_iota(jnp.int32, (gys * rows, width), 1) + r * width
-            hot = jnp.where(idx_col[m] == dof, F32(1.0), F32(0.0)).astype(BF16)
-            gat[m, :, r * width:(r + 1) * width] = hot
+        for c in range(gys):
+            value = jnp.zeros((cap, lanes), jnp.int32)
+            for t in range(cap):
+                value = jnp.where(slot == t, node_of(m, c, t), value)
+            wanted = jnp.concatenate(
+                [jnp.where(value >= 0, value * DOFS + d, -1) for d in range(DOFS)], axis=0)
+            lane = lax.broadcasted_iota(jnp.int32, (rows, lanes), 1)
+            for b in range(nb * width // lanes):
+                hot = jnp.where(wanted == lane + b * lanes, F32(1.0), F32(0.0)).astype(BF16)
+                gat[m, c * rows:(c + 1) * rows, b * lanes:(b + 1) * lanes] = hot
         return carry
 
     lax.fori_loop(0, members, gather_matrix, 0)
 
     for r in order[:4]:
-        pltpu.make_async_copy(v_hbm.at[r], v32.at[r], v_sem.at[r]).wait()
-        ext[0][r] = v32[r].astype(BF16)
+        pltpu.make_async_copy(v_hbm.at[r], acc0.at[r], v_sem.at[r]).wait()
+        ext[0][r] = acc0[r].astype(BF16)
 
     pl.semaphore_wait(barrier, gys - 1 + groups * gxs - 1 + jnp.where(rod, chunks, gys))
 
@@ -140,8 +157,8 @@
             kap_copy(c, my_chunk).start()
 
     for r in order[4:]:
-        pltpu.make_async_copy(v_hbm.at[r], v32.at[r], v_sem.at[r]).wait()
-        ext[0][r] = v32[r].astype(BF16)
+        pltpu.make_async_copy(v_hbm.at[r], acc0.at[r], v_sem.at[r]).wait()
+        ext[0][r] = acc0[r].astype(BF16)
 
     def gather(s):
         def one(m, carry):
@@ -157,7 +174,7 @@
             acc0[r] = jnp.dot(a[r, 0], ext[s][r], preferred_element_type=F32)
             return carry
 
-        lax.fori_loop(0, nb, one, 0)
+        lax.fori_loop(0, nb, one, 0, unroll=4)
 
     def spring_forces(s):
         each_chunk(lambda c: sleeve_copy(s, c, c).wait_recv())
@@ -172,7 +189,7 @@
                 pltpu.make_async_copy(
                     a_hbm.at[r, pl.ds(1, kb - 1)], a.at[r, pl.ds(1, kb - 1)], a_sem.at[r]).wait()
             left = jnp.concatenate([a[r, k] for k in range(1, kb)] + [sca[r]], axis=1)
-            right = jnp.concatenate([ext[s][cols[r * kb + k]] for k in range(1, kb)] + [dlt[...]], axis=0)
+            right = jnp.concatenate([ext[s][cols[k, r]] for k in range(1, kb)] + [dlt[...]], axis=0)
             c = acc0[r] + jnp.dot(left, right, preferred_element_type=F32)
             if s > 0:
                 c = c * inv[...]
@@ -181,10 +198,9 @@
                 ext[s + 1][r] = c.astype(BF16)
             else:
                 c3[r] = c
-                pltpu.make_async_copy(c3.at[r], out_hbm.at[r], o_sem.at[r]).start()
             return carry
 
-        lax.fori_loop(start, stop, one, 0)
+        lax.fori_loop(start, stop, one, 0, unroll=2)
 
     def line_copy(s, i, slot):
         return pltpu.make_async_remote_copy(
@@ -230,13 +246,28 @@
         scale = jnp.sqrt(jnp.sum(total, axis=0, keepdims=True) / all_dofs + EPSILON)
         norms[s:s + 1, :] = scale
         inv[...] = 1.0 / scale
+        if s == MATVECS - 1:
+            inverse[...] = 1.0 / scale
 
     for s in range(MATVECS):
         gather(s)
         if s == 0:
+            padded = sca.shape[2]
+            place = lax.broadcasted_iota(jnp.int32, (8, padded), 1)
+            within = lax.rem(place, rows)
+            key = lax.div(place, rows) * cap + lax.rem(within, cap)
+
+            def slot_row(j, value):
+                c = lax.div(j, cap)
+                node = node_of(lax.div(c, gys), lax.rem(c, gys), lax.rem(j, cap))
+                return jnp.where(key == j, node, value)
+
+            node_row = lax.fori_loop(0, chunks * cap, slot_row, jnp.full((8, padded), -1, jnp.int32))
+            node_row = jnp.where(node_row >= 0, node_row * DOFS + lax.div(within, cap), -1)
+
             def scatter_matrix(r, carry):
-                dof = lax.broadcasted_iota(jnp.int32, (width, sca.shape[2]), 0) + r * width
-                sca[r] = jnp.where(idx_row[...] == dof, F32(1.0), F32(0.0)).astype(BF16)
+                dof = lax.broadcasted_iota(jnp.int32, (width, padded), 0) + r * width
+                sca[r] = jnp.where(node_row[:1] == dof, F32(1.0), F32(0.0)).astype(BF16)
                 return carry
 
             lax.fori_loop(0, nb, scatter_matrix, 0)
@@ -278,8 +309,6 @@
         for c in range(gys):
             kap_copy(c, c).wait_send()
 
-    for r in range(nb):
-        pltpu.make_async_copy(c3.at[r], out_hbm.at[r], o_sem.at[r]).wait()
     squares_end(MATVECS - 1)
     for s in range(MATVECS):
         for p in range(groups * gxs):
@@ -297,35 +326,24 @@
     chunks = members * gys
     slot_rows = chunks * rows
     padded = -(-slot_rows // 256) * 256
-    g = lax.axis_index("group")
-    member = jnp.maximum(g - 1, 0)
-    memb = lax.dynamic_index_in_dim(sleeve_membrane[0, :, :, 0, :], member, axis=1, keepdims=False).reshape(-1)
-    stiff = lax.dynamic_index_in_dim(sleeve_stiffness[0, :, :, 0, :], member, axis=1, keepdims=False).reshape(-1)
-    memb = jnp.pad(memb, (0, (members - 1) * gys * cap), constant_values=-1)
-    nodes = jnp.where(g == 0, sleeve_rod[0, 0].reshape(-1), memb)
-    index = jnp.where(nodes[:, None] >= 0, nodes[:, None] * DOFS + jnp.arange(DOFS, dtype=jnp.int32)[None, :], -1)
-    index = index.reshape(-1)
-    idx_col = index.reshape(members, gys * rows, 1)
-    idx_row = jnp.pad(index, (0, padded - slot_rows), constant_values=-1).reshape(1, padded)
-    kap_col = jnp.broadcast_to(stiff[:, None], (gys * cap, DOFS)).reshape(gys * rows, 1)
+    smem = pl.BlockSpec(memory_space=pltpu.SMEM)
     vmem = pl.BlockSpec(memory_space=pltpu.VMEM)
     hbm = pl.BlockSpec(memory_space=pl.ANY)
     dma = pltpu.SemaphoreType.DMA
     plane = groups * gxs
     flops = 2 * MATVECS * nb * kb * width * width * lanes
-    coupled, norms = pl.pallas_call(
+    coupled, norms, inverse = pl.pallas_call(
         functools.partial(kernel, groups, gxs, gys, nb, kb, width, lanes, rows),
         out_shape=(
-            jax.ShapeDtypeStruct((nb, width, lanes), F32),
+            pltpu.VMEM((nb, width, lanes), F32),
             jax.ShapeDtypeStruct((MATVECS, lanes), F32),
+            jax.ShapeDtypeStruct((1, lanes), F32),
         ),
-        in_specs=[pl.BlockSpec(memory_space=pltpu.SMEM), vmem, vmem, vmem, hbm, hbm],
-        out_specs=(hbm, vmem),
+        in_specs=[smem, smem, smem, smem, hbm, hbm],
+        out_specs=(vmem, vmem, vmem),
         scratch_shapes=[
             pltpu.VMEM((nb, kb, width, width), BF16),
             *[pltpu.VMEM((nb + 4, width, lanes), BF16)] * MATVECS,
-            pltpu.VMEM((nb, width, lanes), F32),
-            pltpu.VMEM((nb, width, lanes), F32),
             pltpu.VMEM((nb, width, lanes), F32),
             pltpu.VMEM((members, gys * rows, nb * width), BF16),
             pltpu.VMEM((nb, width, padded), BF16),
@@ -338,7 +356,7 @@
             pltpu.VMEM((MATVECS, gys, 8, lanes), F32),
             pltpu.VMEM((MATVECS, plane, 8, lanes), F32),
             pltpu.VMEM((1, lanes), F32),
-            dma((nb,)), dma, dma((nb,)), dma((nb,)),
+            dma((nb,)), dma, dma((nb,)),
             dma((MATVECS, 4)), dma((MATVECS, 4)),
             dma((MATVECS, chunks)), dma((MATVECS, chunks)),
             dma((gys,)), dma((chunks,)),
@@ -346,11 +364,11 @@
             dma((MATVECS, plane)), dma((MATVECS, plane)),
         ],
         compiler_params=pltpu.CompilerParams(
-            collective_id=0, has_side_effects=True, vmem_limit_bytes=60 * 2**20),
+            collective_id=0, has_side_effects=True, vmem_limit_bytes=58 * 2**20),
         cost_estimate=pl.CostEstimate(flops=flops, bytes_accessed=tile_blocks.size * 2, transcendentals=0),
-    )(block_columns.reshape(-1), idx_col, idx_row, kap_col,
+    )(block_columns[0, 0, 0].T, sleeve_rod[0, 0], sleeve_membrane[0], sleeve_stiffness[0],
       start_vectors.reshape(nb, width, lanes), tile_blocks.reshape(nb, kb, width, width))
-    final = coupled / norms[MATVECS - 1]
+    final = coupled * inverse
     return (final[None, None, None], norms)
 
 

time: 60.2 us -> 50.6 us (0.84)
  local copies, waits for them, and re-layouts: 6.84 us -> 0.58 us
  other arithmetic: 5.44 us -> 1.91 us
    unnamed x2 -> x0, other arithmetic: 2.69 us -> none
    unnamed x6 -> x3, local copies, waits for them, and re-layouts: 2.36 us -> 0.58 us
    reshape x3 -> x0, local copies, waits for them, and re-layouts: 1.46 us -> none  [the longest x1 0.72 us: local(): jnp.broadcast_to(stiff[:, None], (gys * cap, DOFS)).reshape(gys * rows, 1)]
    select_n x2 -> x0, local copies, waits for them, and re-layouts: 0.84 us -> none  [local(): jnp.where(nodes[:, None] >= 0, nodes[:, None] * DOFS + jnp.arange(DOFS, d...]
    another operation x1 -> x0, local copies, waits for them, and re-layouts: 0.76 us -> none  [local(): nodes = jnp.where(g == 0, sleeve_rod[0, 0].reshape(-1), memb)]
    broadcast_in_dim x1, other arithmetic: 2.66 us -> 1.91 us  [local(): return (final[None, None, None], norms)]
    div x1 -> x0, local copies, waits for them, and re-layouts: 0.69 us -> none  [local(): final = coupled / norms[MATVECS - 1]]
where the time goes in v2:
time: 50.6 us; the launch traced here: 50.4 us
  Pallas kernels  47.2 us (93%)
  other arithmetic  1.91 us (4%)
  between operations  0.65 us (1%)
  local copies, waits for them, and re-layouts  0.58 us (1%)
    pallas_call x1, Pallas kernels, local(): pl.pallas_call(functools.partial(kernel, groups, gxs, gys, nb, kb, width,...  47.2 us
    broadcast_in_dim x1, other arithmetic, local(): return (final[None, None, None], norms)  1.91 us

profile of v2, /device:TPU:0, one launch (start us, length us, event | category | flops | bytes accessed | tf_op | source)
XLA Modules:
  0.0 50.4 jit_solution(7752924132638081648)
XLA Ops:
  0.6 47.2 %shard_map.77 = (f32[8,384,128]{2,1,0:T(8,128)S(1)}, f32[3,128]{1,0:T(4,128)}, f32[1,128]{1,0:T(1,128)}) custom-call(s32[4,8]{1,0:T(4,128)} %bitcast.18, s32[1,4,8]{2,1,0:T(4,128)} %bitcast.19, s32[4,1,1,8]{3,2,1,0:T(1,128)} %bitcast.20, f32[4,1,1,8]{3,2,1,0:T(1,128)} %bitcast.21, f32[8,384,128]{2,1,0:T(8,128)} %bitcast.17, bf16[8,4,384,384]{3,2,1,0:T(8,128)(2,1)} %bitcast.16), custom_call_target="tpu_custom_call" | custom-call | flops 3623878656 | bytes 9437184 | tf_op jit(solution)/shard_map/pallas_call | solution.py:335
  47.9 0.0 copy-start
  47.9 1.9 %multiply_bitcast_fusion = f32[1,1,1,8,384,128]{5,4,3,2,1,0:T(8,128)} fusion(f32[8,384,128]{2,1,0:T(8,128)S(1)} %get-tuple-element.5, f32[128]{0:T(128)} %bitcast.15), kind=kLoop, calls=%fused_computation | loop fusion | flops 393216 | bytes 3146240 | tf_op jit(solution)/shard_map/broadcast_in_dim | solution.py:372
  49.8 0.0 copy-done
  49.8 0.6 %copy.11 = f32[3,128]{1,0:T(4,128)} copy(f32[3,128]{1,0:T(4,128)S(1)} %copy-done) | data formatting | bytes 3072
Async XLA Ops:
  47.9 1.9 %copy-start = (f32[3,128]{1,0:T(4,128)S(1)}, f32[3,128]{1,0:T(4,128)}, u32[]{:S(2)}) copy-start(f32[3,128]{1,0:T(4,128)} %get-tuple-element.11) | copy-start | bytes 4612

commit v3 on v2

v3 whole, which is shorter than its diff:
```python
import functools

import jax
import jax.numpy as jnp
from jax import lax
from jax.experimental import pallas as pl
from jax.experimental.pallas import tpu as pltpu
from jax.sharding import PartitionSpec as P

MATVECS = 3
DOFS = 6
EPSILON = 1e-06
MESH = pl.DeviceIdType.MESH
F32 = jnp.float32
BF16 = jnp.bfloat16


def kernel(groups, gxs, gys, nb, kb, width, lanes, rows,
           cols_hbm, rod_hbm, memb_hbm, stiff_hbm, v_hbm, a_hbm,
           result, norms,
           cols, rod_nodes, memb_nodes, stiff, a, ext, land, acc0, gat, sca, own, oth, kown, kap, dlt, sqacc, sqa, sqb, inv,
           i_sem, v_sem, a0_sem, a_sem, gs, gr, ss, sr, ks, kr, as_, ar, bs, br):
    g = lax.axis_index("group")
    x = lax.axis_index("gx")
    y = lax.axis_index("gy")
    plane = g * gxs + x
    rod = g == 0
    members = groups - 1
    chunks = members * gys
    all_dofs = float(groups * gxs * gys * nb * width)

    def row_of(i):
        half, odd = lax.div(i, 2), lax.rem(i, 2)
        return half * (1 - 2 * odd) + odd * (nb - 1)

    order = [i // 2 if i % 2 == 0 else nb - 1 - i // 2 for i in range(nb)]
    for r in order:
        pltpu.make_async_copy(v_hbm.at[r], acc0.at[r], v_sem.at[r]).start()
    pltpu.make_async_copy(a_hbm.at[:, 0], a.at[:, 0], a0_sem).start()
    for r in order:
        pltpu.make_async_copy(a_hbm.at[r, pl.ds(1, kb - 1)], a.at[r, pl.ds(1, kb - 1)], a_sem.at[r]).start()

    small = [
        pltpu.make_async_copy(src, dst, i_sem.at[i])
        for i, (src, dst) in enumerate(
            ((rod_hbm, rod_nodes), (memb_hbm, memb_nodes), (stiff_hbm, stiff), (cols_hbm, cols)))
    ]
    for copy in small:
        copy.start()

    barrier = pltpu.get_barrier_semaphore()
    for i in range(gys):
        @pl.when(i != y)
        def _():
            pl.semaphore_signal(barrier, inc=1, device_id=(g, x, i), device_id_type=MESH)
    for p in range(groups * gxs):
        @pl.when(p != plane)
        def _():
            pl.semaphore_signal(barrier, inc=1, device_id=(p // gxs, p % gxs, y), device_id_type=MESH)

    def peer(c):
        return (jnp.where(rod, c // gys + 1, 0), x, c % gys)

    def each_chunk(body):
        for c in range(chunks):
            if c < gys:
                body(c)
            else:
                pl.when(rod)(functools.partial(body, c))

    each_chunk(lambda c: pl.semaphore_signal(barrier, inc=1, device_id=peer(c), device_id_type=MESH))

    sides = (
        (nb - 1, x < gxs - 1, lambda: (g, x + 1, y), x > 0, lambda: (g, x - 1, y)),
        (0, x > 0, lambda: (g, x - 1, y), x < gxs - 1, lambda: (g, x + 1, y)),
        (1, y < gys - 1, lambda: (g, x, y + 1), y > 0, lambda: (g, x, y - 1)),
        (nb - 2, y > 0, lambda: (g, x, y - 1), y < gys - 1, lambda: (g, x, y + 1)),
    )
    for r in order[:4]:
        pltpu.make_async_copy(v_hbm.at[r], acc0.at[r], v_sem.at[r]).wait()
        ext[0, r] = acc0[r].astype(BF16)

    pl.semaphore_wait(barrier, gys - 1 + groups * gxs - 1 + jnp.where(rod, chunks, gys))

    def side_copy(s, d, device):
        return pltpu.make_async_remote_copy(
            src_ref=ext.at[lax.rem(s, 2), sides[d][0]], dst_ref=land.at[s, d],
            send_sem=gs.at[s, d], recv_sem=gr.at[s, d],
            device_id=device, device_id_type=MESH)

    def send_sides(s, more=True):
        for d, (_, sends, to, _, _) in enumerate(sides):
            @pl.when(sends & more)
            def _():
                side_copy(s, d, to()).start()

    def wait_sides(s):
        for d, (_, _, _, hears, source) in enumerate(sides):
            @pl.when(hears)
            def _():
                side_copy(s, d, source()).wait_recv()
        for d, (_, sends, to, _, _) in enumerate(sides):
            ext[lax.rem(s, 2), nb + d] = land[s, d]

            @pl.when(sends)
            def _():
                side_copy(s, d, to()).wait_send()

    my_chunk = jnp.where(rod, y, (g - 1) * gys + y)

    def sleeve_copy(s, c, dst):
        return pltpu.make_async_remote_copy(
            src_ref=own.at[s, c // gys, c % gys], dst_ref=oth.at[s, dst // gys, dst % gys],
            send_sem=ss.at[s, c], recv_sem=sr.at[s, dst],
            device_id=peer(c), device_id_type=MESH)

    def kap_copy(c, dst):
        return pltpu.make_async_remote_copy(
            src_ref=kown.at[c % gys], dst_ref=kap.at[dst // gys, dst % gys],
            send_sem=ks.at[c % gys], recv_sem=kr.at[dst],
            device_id=peer(c), device_id_type=MESH)

    send_sides(0)
    for copy in small:
        copy.wait()

    for d, (_, _, _, hears, _) in enumerate(sides):
        @pl.when(jnp.logical_not(hears))
        def _():
            for s in range(MATVECS):
                land[s, d] = jnp.zeros((width, lanes), BF16)

    cap = rows // DOFS
    member = jnp.maximum(g - 1, 0)
    slot = lax.broadcasted_iota(jnp.int32, (cap, lanes), 0)
    for c in range(gys):
        value = jnp.zeros((cap, lanes), F32)
        for t in range(cap):
            value = jnp.where(slot == t, stiff[c, member, 0, t], value)
        for d in range(DOFS):
            kown[c, d * cap:(d + 1) * cap] = value

    @pl.when(jnp.logical_not(rod))
    def _():
        kap[0] = kown[...]
        for m in range(1, members):
            kap[m] = jnp.zeros((gys, rows, lanes), F32)
            for s in range(MATVECS):
                oth[s, m] = jnp.zeros((gys, rows, lanes), BF16)

    def node_of(m, c, t):
        return jnp.where(rod, rod_nodes[m, c, t], jnp.where(m == 0, memb_nodes[c, member, 0, t], -1))

    def gather_matrix(m, carry):
        for c in range(gys):
            value = jnp.zeros((cap, lanes), jnp.int32)
            for t in range(cap):
                value = jnp.where(slot == t, node_of(m, c, t), value)
            wanted = jnp.concatenate(
                [jnp.where(value >= 0, value * DOFS + d, -1) for d in range(DOFS)], axis=0)
            lane = lax.broadcasted_iota(jnp.int32, (rows, lanes), 1)
            for b in range(nb * width // lanes):
                hot = jnp.where(wanted == lane + b * lanes, F32(1.0), F32(0.0)).astype(BF16)
                gat[m, c * rows:(c + 1) * rows, b * lanes:(b + 1) * lanes] = hot
        return carry

    lax.fori_loop(0, members, gather_matrix, 0)


    @pl.when(jnp.logical_not(rod))
    def _():
        for c in range(gys):
            kap_copy(c, my_chunk).start()

    for r in order[4:]:
        pltpu.make_async_copy(v_hbm.at[r], acc0.at[r], v_sem.at[r]).wait()
        ext[0, r] = acc0[r].astype(BF16)

    def gather(s):
        def one(m, carry):
            got = jnp.dot(gat[m], ext[lax.rem(s, 2), :nb].reshape(nb * width, lanes), preferred_element_type=F32)
            own[s, m] = got.astype(BF16).reshape(gys, rows, lanes)
            return carry

        lax.fori_loop(0, members, one, 0)
        each_chunk(lambda c: sleeve_copy(s, c, my_chunk).start())

    early = width // 256 * 256

    def first_blocks(s):
        def one(r, carry):
            acc0[r] = jnp.dot(a[r, 0, :, :early], ext[lax.rem(s, 2), r, :early], preferred_element_type=F32)
            return carry

        lax.fori_loop(0, nb, one, 0, unroll=4)

    def spring_forces(s):
        each_chunk(lambda c: sleeve_copy(s, c, c).wait_recv())
        for m in range(members):
            force = kap[m] * (own[s, m].astype(F32) - oth[s, m].astype(F32))
            dlt[m * gys * rows:(m + 1) * gys * rows] = force.astype(BF16).reshape(gys * rows, lanes)

    def main_rows(s, half):
        now = lax.rem(s, 2)

        def one(i, carry):
            r = row_of(half * 4 + i)
            left = jnp.concatenate(
                [a[r, 0, :, early:]] + [a[r, k] for k in range(1, kb)] + [sca[r]], axis=1)
            right = jnp.concatenate(
                [ext[now, r, early:]] + [ext[now, cols[k, r]] for k in range(1, kb)] + [dlt[...]], axis=0)
            c = (acc0[r] + jnp.dot(left, right, preferred_element_type=F32)) * inv[...]
            sqacc[...] += jnp.sum((c * c).reshape(width // 8, 8, lanes), axis=0)
            ext[1 - now, r] = c.astype(BF16)
            acc0[r] = c
            return carry

        lax.fori_loop(0, 4, one, 0, unroll=2)

    def line_copy(s, i, slot):
        return pltpu.make_async_remote_copy(
            src_ref=sqa.at[s, y], dst_ref=sqa.at[s, slot],
            send_sem=as_.at[s, i], recv_sem=ar.at[s, slot],
            device_id=(g, x, i), device_id_type=MESH)

    def plane_copy(s, p, slot):
        return pltpu.make_async_remote_copy(
            src_ref=sqb.at[s, plane], dst_ref=sqb.at[s, slot],
            send_sem=bs.at[s, p], recv_sem=br.at[s, slot],
            device_id=(p // gxs, p % gxs, y), device_id_type=MESH)

    def squares_line(s):
        sqa[s, y] = sqacc[...]
        for i in range(gys):
            @pl.when(i != y)
            def _():
                line_copy(s, i, y).start()

    def squares_plane(s):
        for i in range(gys):
            @pl.when(i != y)
            def _():
                line_copy(s, i, i).wait_recv()
        total = sqa[s, 0]
        for i in range(1, gys):
            total = total + sqa[s, i]
        sqb[s, plane] = total
        for p in range(groups * gxs):
            @pl.when(p != plane)
            def _():
                plane_copy(s, p, plane).start()

    def squares_end(s):
        for p in range(groups * gxs):
            @pl.when(p != plane)
            def _():
                plane_copy(s, p, p).wait_recv()
        total = sqb[s, 0]
        for p in range(1, groups * gxs):
            total = total + sqb[s, p]
        scale = jnp.sqrt(jnp.sum(total, axis=0, keepdims=True) / all_dofs + EPSILON)
        norms[pl.ds(s, 1), :] = scale
        inv[...] = 1.0 / scale

    padded = sca.shape[2]
    place = lax.broadcasted_iota(jnp.int32, (8, padded), 1)
    within = lax.rem(place, rows)
    key = lax.div(place, rows) * cap + lax.rem(within, cap)

    def slot_row(j, value):
        c = lax.div(j, cap)
        node = node_of(lax.div(c, gys), lax.rem(c, gys), lax.rem(j, cap))
        return jnp.where(key == j, node, value)

    node_row = lax.fori_loop(0, chunks * cap, slot_row, jnp.full((8, padded), -1, jnp.int32))
    node_row = jnp.where(node_row >= 0, node_row * DOFS + lax.div(within, cap), -1)

    def scatter_matrix(r, carry):
        dof = lax.broadcasted_iota(jnp.int32, (width, padded), 0) + r * width
        sca[r] = jnp.where(node_row[:1] == dof, F32(1.0), F32(0.0)).astype(BF16)
        return carry

    lax.fori_loop(0, nb, scatter_matrix, 0)
    if dlt.shape[0] > chunks * rows:
        dlt[chunks * rows:] = jnp.zeros((dlt.shape[0] - chunks * rows, lanes), BF16)
    inv[...] = jnp.ones_like(inv)
    last = MATVECS - 1

    def step(s, carry):
        gather(s)

        @pl.when(s == 0)
        def _():
            pltpu.make_async_copy(a_hbm.at[:, 0], a.at[:, 0], a0_sem).wait()

        first_blocks(s)

        @pl.when(s > 0)
        def _():
            squares_plane(s - 1)

        @pl.when((s == 0) & rod)
        def _():
            for c in range(chunks):
                kap_copy(c, c).wait_recv()

        spring_forces(s)
        wait_sides(s)

        @pl.when(s > 0)
        def _():
            squares_end(s - 1)

        @pl.when(s == 0)
        def _():
            for r in order:
                pltpu.make_async_copy(
                    a_hbm.at[r, pl.ds(1, kb - 1)], a.at[r, pl.ds(1, kb - 1)], a_sem.at[r]).wait()

        sqacc[...] = jnp.zeros_like(sqacc)

        def part(half, carry):
            main_rows(s, half)
            send_sides(s + 1, (half == 0) & (s < last))
            return carry

        lax.fori_loop(0, nb // 4, part, 0)
        squares_line(s)
        return carry

    lax.fori_loop(0, MATVECS, step, 0)
    squares_plane(last)

    def sent(s, carry):
        each_chunk(lambda c: sleeve_copy(s, c, c).wait_send())
        for i in range(gys):
            @pl.when(i != y)
            def _():
                line_copy(s, i, y).wait_send()
        for p in range(groups * gxs):
            @pl.when(p != plane)
            def _():
                plane_copy(s, p, plane).wait_send()
        return carry

    lax.fori_loop(0, MATVECS, sent, 0)

    @pl.when(jnp.logical_not(rod))
    def _():
        for c in range(gys):
            kap_copy(c, c).wait_send()

    squares_end(last)
    for r in range(nb):
        result[r] = acc0[r] * inv[...]


def local(groups, gxs, gys, start_vectors, tile_blocks, block_columns, sleeve_rod, sleeve_membrane, sleeve_stiffness):
    nb, kb, width = tile_blocks.shape[3:6]
    lanes = start_vectors.shape[5]
    cap = sleeve_rod.shape[4]
    members = groups - 1
    rows = cap * DOFS
    chunks = members * gys
    slot_rows = chunks * rows
    padded = -(-slot_rows // 256) * 256
    small = (block_columns[0, 0, 0].T, sleeve_rod[0, 0], sleeve_membrane[0], sleeve_stiffness[0])
    vmem = pl.BlockSpec(memory_space=pltpu.VMEM)
    hbm = pl.BlockSpec(memory_space=pl.ANY)
    dma = pltpu.SemaphoreType.DMA
    plane = groups * gxs
    flops = 2 * MATVECS * nb * kb * width * width * lanes
    final, norms = pl.pallas_call(
        functools.partial(kernel, groups, gxs, gys, nb, kb, width, lanes, rows),
        out_shape=(
            pltpu.VMEM((nb, width, lanes), F32),
            pltpu.VMEM((MATVECS, lanes), F32),
        ),
        in_specs=[hbm] * 6,
        out_specs=(vmem, vmem),
        scratch_shapes=[
            *[pltpu.SMEM(array.shape, array.dtype) for array in small],
            pltpu.VMEM((nb, kb, width, width), BF16),
            pltpu.VMEM((2, nb + 4, width, lanes), BF16),
            pltpu.VMEM((MATVECS, 4, width, lanes), BF16),
            pltpu.VMEM((nb, width, lanes), F32),
            pltpu.VMEM((members, gys * rows, nb * width), BF16),
            pltpu.VMEM((nb, width, padded), BF16),
            pltpu.VMEM((MATVECS, members, gys, rows, lanes), BF16),
            pltpu.VMEM((MATVECS, members, gys, rows, lanes), BF16),
            pltpu.VMEM((gys, rows, lanes), F32),
            pltpu.VMEM((members, gys, rows, lanes), F32),
            pltpu.VMEM((padded, lanes), BF16),
            pltpu.VMEM((8, lanes), F32),
            pltpu.VMEM((MATVECS, gys, 8, lanes), F32),
            pltpu.VMEM((MATVECS, plane, 8, lanes), F32),
            pltpu.VMEM((1, lanes), F32),
            dma((4,)), dma((nb,)), dma, dma((nb,)),
            dma((MATVECS, 4)), dma((MATVECS, 4)),
            dma((MATVECS, chunks)), dma((MATVECS, chunks)),
            dma((gys,)), dma((chunks,)),
            dma((MATVECS, gys)), dma((MATVECS, gys)),
            dma((MATVECS, plane)), dma((MATVECS, plane)),
        ],
        compiler_params=pltpu.CompilerParams(
            collective_id=0, has_side_effects=True, vmem_limit_bytes=58 * 2**20),
        cost_estimate=pl.CostEstimate(flops=flops, bytes_accessed=tile_blocks.size * 2, transcendentals=0),
    )(*small,
      start_vectors.reshape(nb, width, lanes), tile_blocks.reshape(nb, kb, width, width))
    return (final[None, None, None], norms)


def solution(mesh):
    return jax.shard_map(
        functools.partial(local, mesh.shape["group"], mesh.shape["gx"], mesh.shape["gy"]),
        mesh=mesh,
        in_specs=(
            P("group", "gx", "gy", None, None, None),
            P("group", "gx", "gy", None, None, None, None),
            P("group", "gx", "gy", None, None),
            P("gx", "gy", None, None, None),
            P("gx", None, None, "gy", None),
            P("gx", None, None, "gy", None),
        ),
        out_specs=(P("group", "gx", "gy", None, None, None), P()),
        check_vma=False,
    )
```

time: 50.6 us -> 48.7 us (0.962)
  other arithmetic: 1.91 us -> 0 us
  local copies, waits for them, and re-layouts: 0.58 us -> 1.72 us
  Pallas kernels: 47.2 us -> 46.2 us
    broadcast_in_dim x1 -> x0, other arithmetic: 1.91 us -> none  [local(): return (final[None, None, None], norms)]
    unnamed x3 -> x2, local copies, waits for them, and re-layouts: 0.58 us -> 1.72 us
    pallas_call x1, Pallas kernels: 47.2 us -> 46.2 us  [local(): pl.pallas_call(functools.partial(kernel, groups, gxs, gys, nb, kb, width,...]
where the time goes in v3:
time: 48.7 us; the launch traced here: 48.5 us
  Pallas kernels  46.2 us (95%)
  local copies, waits for them, and re-layouts  1.72 us (4%)
  between operations  0.64 us (1%)
    pallas_call x1, Pallas kernels, local(): pl.pallas_call(functools.partial(kernel, groups, gxs, gys, nb, kb, width,...  46.2 us
    unnamed x2, local copies, waits for them, and re-layouts  1.72 us

profile of v3, /device:TPU:0, one launch (start us, length us, event | category | flops | bytes accessed | tf_op | source)
XLA Modules:
  0.0 48.5 jit_solution(2550914432535253676)
XLA Ops:
  0.6 46.2 %shard_map.77 = (f32[8,384,128]{2,1,0:T(8,128)S(1)}, f32[3,128]{1,0:T(4,128)S(1)}) custom-call(s32[4,8]{1,0:T(4,128)} %bitcast.16, s32[1,4,8]{2,1,0:T(4,128)} %bitcast.17, s32[4,1,1,8]{3,2,1,0:T(1,128)} %bitcast.18, f32[4,1,1,8]{3,2,1,0:T(1,128)} %bitcast.19, f32[8,384,128]{2,1,0:T(8,128)} %bitcast.15, bf16[8,4,384,384]{3,2,1,0:T(8,128)(2,1)} %bitcast.14), custom_call_target="tpu_custom_call" | custom-call | flops 3623878656 | bytes 9437184 | tf_op jit(solution)/shard_map/pallas_call | solution.py:373
  46.8 1.1 %copy.12 = f32[1,1,1,8,384,128]{5,4,3,2,1,0:T(8,128)} copy(f32[1,1,1,8,384,128]{5,4,3,2,1,0:T(8,128)S(1)} %bitcast.13) | data formatting | bytes 3145728
  47.9 0.6 %copy.13 = f32[3,128]{1,0:T(4,128)} copy(f32[3,128]{1,0:T(4,128)S(1)} %get-tuple-element.7) | data formatting | bytes 3072

commit v4 on v3

--- a/solution.py
+++ b/solution.py
@@ -18,8 +18,8 @@
 def kernel(groups, gxs, gys, nb, kb, width, lanes, rows,
            cols_hbm, rod_hbm, memb_hbm, stiff_hbm, v_hbm, a_hbm,
            result, norms,
-           cols, rod_nodes, memb_nodes, stiff, a, ext, land, acc0, gat, sca, own, oth, kown, kap, dlt, sqacc, sqa, sqb, inv,
-           i_sem, v_sem, a0_sem, a_sem, gs, gr, ss, sr, ks, kr, as_, ar, bs, br):
+           cols, rod_nodes, memb_nodes, stiff, a, ext, land, rel, acc0, gat, sca, own, oth, kown, kap, dlt, sqacc, sqa, sqb, inv,
+           i_sem, v_sem, a0_sem, a_sem, gs, gr, rs, rr, fs, fr, ss, sr, ks, kr, as_, ar, bs, br):
     g = lax.axis_index("group")
     x = lax.axis_index("gx")
     y = lax.axis_index("gy")
@@ -82,29 +82,86 @@
 
     pl.semaphore_wait(barrier, gys - 1 + groups * gxs - 1 + jnp.where(rod, chunks, gys))
 
-    def side_copy(s, d, device):
-        return pltpu.make_async_remote_copy(
-            src_ref=ext.at[lax.rem(s, 2), sides[d][0]], dst_ref=land.at[s, d],
+    relay = groups == 2 and gxs == 4
+    cut = width // 2
+    far = ((x == 1), (x == 2), None, None)
+    far_hears = ((x == 2), (x == 1), None, None)
+
+    def side_copy(s, d, device, part=slice(None)):
+        return pltpu.make_async_remote_copy(
+            src_ref=ext.at[lax.rem(s, 2), sides[d][0], part], dst_ref=land.at[s, d, part],
             send_sem=gs.at[s, d], recv_sem=gr.at[s, d],
             device_id=device, device_id_type=MESH)
 
-    def send_sides(s, more=True):
-        for d, (_, sends, to, _, _) in enumerate(sides):
-            @pl.when(sends & more)
-            def _():
+    def relay_copy(s):
+        return pltpu.make_async_remote_copy(
+            src_ref=ext.at[lax.rem(s, 2), jnp.where(x == 1, nb - 1, 0), pl.ds(cut, cut)], dst_ref=rel.at[s],
+            send_sem=rs.at[s], recv_sem=rr.at[s],
+            device_id=(g, jnp.where(x == 1, 3, jnp.where(x == 2, 0, jnp.where(x == 0, 2, 1))), y),
+            device_id_type=MESH)
+
+    def forward_copy(s):
+        side = jnp.where((x == 3) | (x == 2), 0, 1)
+        return pltpu.make_async_remote_copy(
+            src_ref=rel.at[s], dst_ref=land.at[s, side, pl.ds(cut, cut)],
+            send_sem=fs.at[s], recv_sem=fr.at[s],
+            device_id=(g, jnp.where(x == 3, 2, jnp.where(x == 2, 3, jnp.where(x == 0, 1, 0))), y),
+            device_id_type=MESH)
+
+    middle = (x == 1) | (x == 2)
+
+    def side_case(d, condition, is_far, whole, halved):
+        if relay and d < 2:
+            pl.when(condition & jnp.logical_not(is_far))(whole)
+            pl.when(condition & is_far)(halved)
+        else:
+            pl.when(condition)(whole)
+
+    def send_sides(s, which, more=True):
+        for d in which:
+            _, sends, to, _, _ = sides[d]
+
+            def whole():
                 side_copy(s, d, to()).start()
 
+            def halved():
+                relay_copy(s).start()
+                side_copy(s, d, to(), pl.ds(0, cut)).start()
+
+            side_case(d, sends & more, far[d], whole, halved)
+
+    def forward(s):
+        if relay:
+            @pl.when(jnp.logical_not(middle))
+            def _():
+                relay_copy(s).wait_recv()
+                forward_copy(s).start()
+
     def wait_sides(s):
-        for d, (_, _, _, hears, source) in enumerate(sides):
-            @pl.when(hears)
-            def _():
+        for d, (_, sends, to, hears, source) in enumerate(sides):
+            def whole():
                 side_copy(s, d, source()).wait_recv()
+
+            def halved():
+                side_copy(s, d, source(), pl.ds(0, cut)).wait_recv()
+                forward_copy(s).wait_recv()
+
+            side_case(d, hears, far_hears[d], whole, halved)
         for d, (_, sends, to, _, _) in enumerate(sides):
             ext[lax.rem(s, 2), nb + d] = land[s, d]
 
-            @pl.when(sends)
-            def _():
+            def whole_sent():
                 side_copy(s, d, to()).wait_send()
+
+            def halved_sent():
+                relay_copy(s).wait_send()
+                side_copy(s, d, to(), pl.ds(0, cut)).wait_send()
+
+            side_case(d, sends, far[d], whole_sent, halved_sent)
+        if relay:
+            @pl.when(jnp.logical_not(middle))
+            def _():
+                forward_copy(s).wait_send()
 
     my_chunk = jnp.where(rod, y, (g - 1) * gys + y)
 
@@ -120,7 +177,7 @@
             send_sem=ks.at[c % gys], recv_sem=kr.at[dst],
             device_id=peer(c), device_id_type=MESH)
 
-    send_sides(0)
+    send_sides(0, (0, 1, 2, 3))
     for copy in small:
         copy.wait()
 
@@ -200,11 +257,11 @@
             force = kap[m] * (own[s, m].astype(F32) - oth[s, m].astype(F32))
             dlt[m * gys * rows:(m + 1) * gys * rows] = force.astype(BF16).reshape(gys * rows, lanes)
 
-    def main_rows(s, half):
+    def main_rows(s, pair):
         now = lax.rem(s, 2)
 
         def one(i, carry):
-            r = row_of(half * 4 + i)
+            r = row_of(pair * 2 + i)
             left = jnp.concatenate(
                 [a[r, 0, :, early:]] + [a[r, k] for k in range(1, kb)] + [sca[r]], axis=1)
             right = jnp.concatenate(
@@ -215,7 +272,7 @@
             acc0[r] = c
             return carry
 
-        lax.fori_loop(0, 4, one, 0, unroll=2)
+        lax.fori_loop(0, 2, one, 0, unroll=2)
 
     def line_copy(s, i, slot):
         return pltpu.make_async_remote_copy(
@@ -288,6 +345,7 @@
 
     def step(s, carry):
         gather(s)
+        forward(s)
 
         @pl.when(s == 0)
         def _():
@@ -319,12 +377,13 @@
 
         sqacc[...] = jnp.zeros_like(sqacc)
 
-        def part(half, carry):
-            main_rows(s, half)
-            send_sides(s + 1, (half == 0) & (s < last))
+        def part(pair, carry):
+            main_rows(s, pair)
+            send_sides(s + 1, (0, 1), (pair == 0) & (s < last))
+            send_sides(s + 1, (2, 3), (pair == 1) & (s < last))
             return carry
 
-        lax.fori_loop(0, nb // 4, part, 0)
+        lax.fori_loop(0, nb // 2, part, 0)
         squares_line(s)
         return carry
 
@@ -383,6 +442,7 @@
             pltpu.VMEM((nb, kb, width, width), BF16),
             pltpu.VMEM((2, nb + 4, width, lanes), BF16),
             pltpu.VMEM((MATVECS, 4, width, lanes), BF16),
+            pltpu.VMEM((MATVECS, width // 2, lanes), BF16),
             pltpu.VMEM((nb, width, lanes), F32),
             pltpu.VMEM((members, gys * rows, nb * width), BF16),
             pltpu.VMEM((nb, width, padded), BF16),
@@ -397,6 +457,7 @@
             pltpu.VMEM((1, lanes), F32),
             dma((4,)), dma((nb,)), dma, dma((nb,)),
             dma((MATVECS, 4)), dma((MATVECS, 4)),
+            *[dma((MATVECS,))] * 4,
             dma((MATVECS, chunks)), dma((MATVECS, chunks)),
             dma((gys,)), dma((chunks,)),
             dma((MATVECS, gys)), dma((MATVECS, gys)),

time: 48.7 us -> 49.2 us (1.010)
  Pallas kernels: 46.2 us -> 46.7 us
    pallas_call x1, Pallas kernels: 46.2 us -> 46.7 us  [local(): pl.pallas_call(functools.partial(kernel, groups, gxs, gys, nb, kb, width,...]
where the time goes in v4:
time: 49.2 us; the launch traced here: 49.1 us
  Pallas kernels  46.7 us (95%)
  local copies, waits for them, and re-layouts  1.72 us (3%)
  between operations  0.64 us (1%)
    pallas_call x1, Pallas kernels, local(): pl.pallas_call(functools.partial(kernel, groups, gxs, gys, nb, kb, width,...  46.7 us
    unnamed x2, local copies, waits for them, and re-layouts  1.72 us

profile of v4, /device:TPU:0, one launch (start us, length us, event | category | flops | bytes accessed | tf_op | source)
XLA Modules:
  0.0 49.1 jit_solution(9545242783338030403)
XLA Ops:
  0.6 46.7 %shard_map.77 = (f32[8,384,128]{2,1,0:T(8,128)S(1)}, f32[3,128]{1,0:T(4,128)S(1)}) custom-call(s32[4,8]{1,0:T(4,128)} %bitcast.16, s32[1,4,8]{2,1,0:T(4,128)} %bitcast.17, s32[4,1,1,8]{3,2,1,0:T(1,128)} %bitcast.18, f32[4,1,1,8]{3,2,1,0:T(1,128)} %bitcast.19, f32[8,384,128]{2,1,0:T(8,128)} %bitcast.15, bf16[8,4,384,384]{3,2,1,0:T(8,128)(2,1)} %bitcast.14), custom_call_target="tpu_custom_call" | custom-call | flops 3623878656 | bytes 9437184 | tf_op jit(solution)/shard_map/pallas_call | solution.py:432
  47.4 1.1 %copy.12 = f32[1,1,1,8,384,128]{5,4,3,2,1,0:T(8,128)} copy(f32[1,1,1,8,384,128]{5,4,3,2,1,0:T(8,128)S(1)} %bitcast.13) | data formatting | bytes 3145728
  48.5 0.6 %copy.13 = f32[3,128]{1,0:T(4,128)} copy(f32[3,128]{1,0:T(4,128)S(1)} %get-tuple-element.7) | data formatting | bytes 3072

commit v5 on v3

--- a/solution.py
+++ b/solution.py
@@ -37,8 +37,8 @@
     for r in order:
         pltpu.make_async_copy(v_hbm.at[r], acc0.at[r], v_sem.at[r]).start()
     pltpu.make_async_copy(a_hbm.at[:, 0], a.at[:, 0], a0_sem).start()
-    for r in order:
-        pltpu.make_async_copy(a_hbm.at[r, pl.ds(1, kb - 1)], a.at[r, pl.ds(1, kb - 1)], a_sem.at[r]).start()
+    rest = pltpu.make_async_copy(a_hbm.at[:, pl.ds(1, kb - 1)], a.at[:, pl.ds(1, kb - 1)], a_sem)
+    rest.start()
 
     small = [
         pltpu.make_async_copy(src, dst, i_sem.at[i])
@@ -49,17 +49,22 @@
         copy.start()
 
     barrier = pltpu.get_barrier_semaphore()
-    for i in range(gys):
-        @pl.when(i != y)
-        def _():
-            pl.semaphore_signal(barrier, inc=1, device_id=(g, x, i), device_id_type=MESH)
-    for p in range(groups * gxs):
-        @pl.when(p != plane)
-        def _():
-            pl.semaphore_signal(barrier, inc=1, device_id=(p // gxs, p % gxs, y), device_id_type=MESH)
+    n_plane = groups * gxs
+
+    def line_peer(i):
+        return (g, x, lax.rem(y + i, gys))
+
+    def plane_peer(i):
+        p = lax.rem(plane + i, n_plane)
+        return (lax.div(p, gxs), lax.rem(p, gxs), y)
+
+    for i in range(1, gys):
+        pl.semaphore_signal(barrier, inc=1, device_id=line_peer(i), device_id_type=MESH)
+    for i in range(1, n_plane):
+        pl.semaphore_signal(barrier, inc=1, device_id=plane_peer(i), device_id_type=MESH)
 
     def peer(c):
-        return (jnp.where(rod, c // gys + 1, 0), x, c % gys)
+        return (1 - g if members == 1 else jnp.where(rod, c // gys + 1, 0), x, c % gys)
 
     def each_chunk(body):
         for c in range(chunks):
@@ -111,13 +116,13 @@
     def sleeve_copy(s, c, dst):
         return pltpu.make_async_remote_copy(
             src_ref=own.at[s, c // gys, c % gys], dst_ref=oth.at[s, dst // gys, dst % gys],
-            send_sem=ss.at[s, c], recv_sem=sr.at[s, dst],
+            send_sem=ss.at[s], recv_sem=sr.at[s],
             device_id=peer(c), device_id_type=MESH)
 
     def kap_copy(c, dst):
         return pltpu.make_async_remote_copy(
             src_ref=kown.at[c % gys], dst_ref=kap.at[dst // gys, dst % gys],
-            send_sem=ks.at[c % gys], recv_sem=kr.at[dst],
+            send_sem=ks, recv_sem=kr,
             device_id=peer(c), device_id_type=MESH)
 
     send_sides(0)
@@ -176,6 +181,18 @@
         pltpu.make_async_copy(v_hbm.at[r], acc0.at[r], v_sem.at[r]).wait()
         ext[0, r] = acc0[r].astype(BF16)
 
+    def sleeve_wait(s, how):
+        def over(mine, theirs):
+            how(pltpu.make_async_remote_copy(
+                src_ref=mine, dst_ref=theirs, send_sem=ss.at[s], recv_sem=sr.at[s],
+                device_id=peer(0), device_id_type=MESH))
+
+        if members == 1:
+            over(own.at[s], oth.at[s])
+        else:
+            pl.when(rod)(lambda: over(own.at[s], oth.at[s]))
+            pl.when(jnp.logical_not(rod))(lambda: over(own.at[s, 0], oth.at[s, 0]))
+
     def gather(s):
         def one(m, carry):
             got = jnp.dot(gat[m], ext[lax.rem(s, 2), :nb].reshape(nb * width, lanes), preferred_element_type=F32)
@@ -195,7 +212,7 @@
         lax.fori_loop(0, nb, one, 0, unroll=4)
 
     def spring_forces(s):
-        each_chunk(lambda c: sleeve_copy(s, c, c).wait_recv())
+        sleeve_wait(s, lambda copy: copy.wait_recv())
         for m in range(members):
             force = kap[m] * (own[s, m].astype(F32) - oth[s, m].astype(F32))
             dlt[m * gys * rows:(m + 1) * gys * rows] = force.astype(BF16).reshape(gys * rows, lanes)
@@ -217,44 +234,40 @@
 
         lax.fori_loop(0, 4, one, 0, unroll=2)
 
-    def line_copy(s, i, slot):
+    def line_copy(s, device, slots):
         return pltpu.make_async_remote_copy(
-            src_ref=sqa.at[s, y], dst_ref=sqa.at[s, slot],
-            send_sem=as_.at[s, i], recv_sem=ar.at[s, slot],
-            device_id=(g, x, i), device_id_type=MESH)
-
-    def plane_copy(s, p, slot):
+            src_ref=sqa.at[s, slots], dst_ref=sqa.at[s, slots],
+            send_sem=as_.at[s], recv_sem=ar.at[s],
+            device_id=device, device_id_type=MESH)
+
+    def plane_copy(s, device, slots):
         return pltpu.make_async_remote_copy(
-            src_ref=sqb.at[s, plane], dst_ref=sqb.at[s, slot],
-            send_sem=bs.at[s, p], recv_sem=br.at[s, slot],
-            device_id=(p // gxs, p % gxs, y), device_id_type=MESH)
+            src_ref=sqb.at[s, slots], dst_ref=sqb.at[s, slots],
+            send_sem=bs.at[s], recv_sem=br.at[s],
+            device_id=device, device_id_type=MESH)
+
+    def line_all(s):
+        return line_copy(s, line_peer(1), pl.ds(0, gys - 1))
+
+    def plane_all(s):
+        return plane_copy(s, plane_peer(1), pl.ds(0, n_plane - 1))
 
     def squares_line(s):
         sqa[s, y] = sqacc[...]
-        for i in range(gys):
-            @pl.when(i != y)
-            def _():
-                line_copy(s, i, y).start()
+        for i in range(1, gys):
+            line_copy(s, line_peer(i), y).start()
 
     def squares_plane(s):
-        for i in range(gys):
-            @pl.when(i != y)
-            def _():
-                line_copy(s, i, i).wait_recv()
+        line_all(s).wait_recv()
         total = sqa[s, 0]
         for i in range(1, gys):
             total = total + sqa[s, i]
         sqb[s, plane] = total
-        for p in range(groups * gxs):
-            @pl.when(p != plane)
-            def _():
-                plane_copy(s, p, plane).start()
+        for i in range(1, n_plane):
+            plane_copy(s, plane_peer(i), plane).start()
 
     def squares_end(s):
-        for p in range(groups * gxs):
-            @pl.when(p != plane)
-            def _():
-                plane_copy(s, p, p).wait_recv()
+        plane_all(s).wait_recv()
         total = sqb[s, 0]
         for p in range(1, groups * gxs):
             total = total + sqb[s, p]
@@ -301,8 +314,9 @@
 
         @pl.when((s == 0) & rod)
         def _():
-            for c in range(chunks):
-                kap_copy(c, c).wait_recv()
+            pltpu.make_async_remote_copy(
+                src_ref=kap, dst_ref=kap, send_sem=ks, recv_sem=kr,
+                device_id=peer(0), device_id_type=MESH).wait_recv()
 
         spring_forces(s)
         wait_sides(s)
@@ -313,9 +327,7 @@
 
         @pl.when(s == 0)
         def _():
-            for r in order:
-                pltpu.make_async_copy(
-                    a_hbm.at[r, pl.ds(1, kb - 1)], a.at[r, pl.ds(1, kb - 1)], a_sem.at[r]).wait()
+            rest.wait()
 
         sqacc[...] = jnp.zeros_like(sqacc)
 
@@ -332,23 +344,18 @@
     squares_plane(last)
 
     def sent(s, carry):
-        each_chunk(lambda c: sleeve_copy(s, c, c).wait_send())
-        for i in range(gys):
-            @pl.when(i != y)
-            def _():
-                line_copy(s, i, y).wait_send()
-        for p in range(groups * gxs):
-            @pl.when(p != plane)
-            def _():
-                plane_copy(s, p, plane).wait_send()
+        sleeve_wait(s, lambda copy: copy.wait_send())
+        line_all(s).wait_send()
+        plane_all(s).wait_send()
         return carry
 
     lax.fori_loop(0, MATVECS, sent, 0)
 
     @pl.when(jnp.logical_not(rod))
     def _():
-        for c in range(gys):
-            kap_copy(c, c).wait_send()
+        pltpu.make_async_remote_copy(
+            src_ref=kown, dst_ref=kown, send_sem=ks, recv_sem=kr,
+            device_id=peer(0), device_id_type=MESH).wait_send()
 
     squares_end(last)
     for r in range(nb):
@@ -395,12 +402,11 @@
             pltpu.VMEM((MATVECS, gys, 8, lanes), F32),
             pltpu.VMEM((MATVECS, plane, 8, lanes), F32),
             pltpu.VMEM((1, lanes), F32),
-            dma((4,)), dma((nb,)), dma, dma((nb,)),
+            dma((4,)), dma((nb,)), dma, dma,
             dma((MATVECS, 4)), dma((MATVECS, 4)),
-            dma((MATVECS, chunks)), dma((MATVECS, chunks)),
-            dma((gys,)), dma((chunks,)),
-            dma((MATVECS, gys)), dma((MATVECS, gys)),
-            dma((MATVECS, plane)), dma((MATVECS, plane)),
+            dma((MATVECS,)), dma((MATVECS,)),
+            dma, dma,
+            *[dma((MATVECS,))] * 4,
         ],
         compiler_params=pltpu.CompilerParams(
             collective_id=0, has_side_effects=True, vmem_limit_bytes=58 * 2**20),

time: 48.7 us -> 47.9 us (0.984)
  Pallas kernels: 46.2 us -> 45.4 us
    pallas_call x1, Pallas kernels: 46.2 us -> 45.4 us  [local(): pl.pallas_call(functools.partial(kernel, groups, gxs, gys, nb, kb, width,...]
where the time goes in v5:
time: 47.9 us; the launch traced here: 47.7 us
  Pallas kernels  45.4 us (95%)
  local copies, waits for them, and re-layouts  1.72 us (4%)
  between operations  0.64 us (1%)
    pallas_call x1, Pallas kernels, local(): pl.pallas_call(functools.partial(kernel, groups, gxs, gys, nb, kb, width,...  45.4 us
    unnamed x2, local copies, waits for them, and re-layouts  1.72 us

profile of v5, /device:TPU:0, one launch (start us, length us, event | category | flops | bytes accessed | tf_op | source)
XLA Modules:
  0.0 47.7 jit_solution(14636845638012536385)
XLA Ops:
  0.6 45.4 %shard_map.77 = (f32[8,384,128]{2,1,0:T(8,128)S(1)}, f32[3,128]{1,0:T(4,128)S(1)}) custom-call(s32[4,8]{1,0:T(4,128)} %bitcast.16, s32[1,4,8]{2,1,0:T(4,128)} %bitcast.17, s32[4,1,1,8]{3,2,1,0:T(1,128)} %bitcast.18, f32[4,1,1,8]{3,2,1,0:T(1,128)} %bitcast.19, f32[8,384,128]{2,1,0:T(8,128)} %bitcast.15, bf16[8,4,384,384]{3,2,1,0:T(8,128)(2,1)} %bitcast.14), custom_call_target="tpu_custom_call" | custom-call | flops 3623878656 | bytes 9437184 | tf_op jit(solution)/shard_map/pallas_call | solution.py:380
  46.0 1.1 %copy.12 = f32[1,1,1,8,384,128]{5,4,3,2,1,0:T(8,128)} copy(f32[1,1,1,8,384,128]{5,4,3,2,1,0:T(8,128)S(1)} %bitcast.13) | data formatting | bytes 3145728
  47.1 0.6 %copy.13 = f32[3,128]{1,0:T(4,128)} copy(f32[3,128]{1,0:T(4,128)S(1)} %get-tuple-element.7) | data formatting | bytes 3072

commit v6 on v5

--- a/solution.py
+++ b/solution.py
@@ -222,11 +222,10 @@
 
         def one(i, carry):
             r = row_of(half * 4 + i)
-            left = jnp.concatenate(
-                [a[r, 0, :, early:]] + [a[r, k] for k in range(1, kb)] + [sca[r]], axis=1)
-            right = jnp.concatenate(
-                [ext[now, r, early:]] + [ext[now, cols[k, r]] for k in range(1, kb)] + [dlt[...]], axis=0)
-            c = (acc0[r] + jnp.dot(left, right, preferred_element_type=F32)) * inv[...]
+            c = acc0[r] + jnp.dot(a[r, 0, :, early:], ext[now, r, early:], preferred_element_type=F32)
+            for k in range(1, kb):
+                c = c + jnp.dot(a[r, k], ext[now, cols[k, r]], preferred_element_type=F32)
+            c = (c + jnp.dot(sca[r], dlt[...], preferred_element_type=F32)) * inv[...]
             sqacc[...] += jnp.sum((c * c).reshape(width // 8, 8, lanes), axis=0)
             ext[1 - now, r] = c.astype(BF16)
             acc0[r] = c

time: 47.9 us -> 47.5 us (level)
  no operation moved by 1% of the time
where the time goes in v6:
time: 47.5 us; the launch traced here: 47.4 us
  Pallas kernels  45 us (95%)
  local copies, waits for them, and re-layouts  1.72 us (4%)
  between operations  0.64 us (1%)
    pallas_call x1, Pallas kernels, local(): pl.pallas_call(functools.partial(kernel, groups, gxs, gys, nb, kb, width,...  45 us
    unnamed x2, local copies, waits for them, and re-layouts  1.72 us

profile of v6, /device:TPU:0, one launch (start us, length us, event | category | flops | bytes accessed | tf_op | source)
XLA Modules:
  0.0 47.4 jit_solution(9425202849667838764)
XLA Ops:
  0.6 45.0 %shard_map.77 = (f32[8,384,128]{2,1,0:T(8,128)S(1)}, f32[3,128]{1,0:T(4,128)S(1)}) custom-call(s32[4,8]{1,0:T(4,128)} %bitcast.16, s32[1,4,8]{2,1,0:T(4,128)} %bitcast.17, s32[4,1,1,8]{3,2,1,0:T(1,128)} %bitcast.18, f32[4,1,1,8]{3,2,1,0:T(1,128)} %bitcast.19, f32[8,384,128]{2,1,0:T(8,128)} %bitcast.15, bf16[8,4,384,384]{3,2,1,0:T(8,128)(2,1)} %bitcast.14), custom_call_target="tpu_custom_call" | custom-call | flops 3623878656 | bytes 9437184 | tf_op jit(solution)/shard_map/pallas_call | solution.py:379
  45.7 1.1 %copy.12 = f32[1,1,1,8,384,128]{5,4,3,2,1,0:T(8,128)} copy(f32[1,1,1,8,384,128]{5,4,3,2,1,0:T(8,128)S(1)} %bitcast.13) | data formatting | bytes 3145728
  46.8 0.6 %copy.13 = f32[3,128]{1,0:T(4,128)} copy(f32[3,128]{1,0:T(4,128)S(1)} %get-tuple-element.7) | data formatting | bytes 3072
